TPU v7x, 256 devices: a whole 4x4x8 slice. The times are simulated.
256 devices in a mesh: patch: 64 (over y, x_lo, z), head: 4 (over x_hi, core).
Axes of the slice: x: 4 (x_hi: 2, x_lo: 2; x = x_hi * 2 + x_lo), y: 4, z: 8, core: 2. Of those that a mesh axis runs over, the one named last changes fastest.
Arguments:
- query: bfloat16 [12288, 2560], P('patch', 'head'), may hold values from -12 to 12
- key_fresh: bfloat16 [12288, 2560], P('patch', 'head'), may hold values from -6 to 6
- value_fresh: bfloat16 [12288, 2560], P('patch', 'head'), may hold values from -6 to 6
- key_stale: bfloat16 [12288, 2560], P('patch', 'head'), may hold values from -6 to 6
- value_stale: bfloat16 [12288, 2560], P('patch', 'head'), may hold values from -6 to 6
- out_weight: bfloat16 [2560, 5120], P('head'), may hold values from -0.125 to 0.125
- residual: bfloat16 [12288, 5120], P('patch', 'head'), may hold values from -6 to 6
- gate: bfloat16 [5120], P('head'), may hold values from 0.5 to 1.5
Outputs:
- updated: bfloat16 [12288, 5120], P('patch', 'head')
All inputs are finite; a program needn't handle non-finite values.
Results may differ from a plain program's by a relative error of at most 0.0075.
Values may be sent and summed in bfloat16 or wider, within the bound.
No kernel may reach another device: no remote copies, remote signals or barrier semaphores. Data moves between devices by JAX's collectives and lax.ppermute only.
A program may use at most 128 MiB of HBM per device.

v0:
```python
import math

import jax
import jax.numpy as jnp
from jax import lax
from jax.sharding import PartitionSpec as P

HD = 128


def key_block(row_count):
    block_size = math.gcd(row_count, 2048)
    return block_size


def absorb(carried, queries, key_rows, value_rows):
    running_max, running_sum, weighted = carried
    head_count = queries.shape[1]
    row_count = key_rows.shape[0]
    key_cube = key_rows.reshape(row_count, head_count, HD)
    value_cube = value_rows.reshape(row_count, head_count, HD)
    scores = jnp.einsum(
        "qhd,khd->hqk", queries, key_cube, preferred_element_type=jnp.float32
    ) * HD ** (-0.5)
    new_max = jnp.maximum(running_max, jnp.max(scores, axis=2))
    rescale = jnp.exp(running_max - new_max)
    weights = jnp.exp(scores - new_max[:, :, None])
    running_sum = running_sum * rescale + jnp.sum(weights, axis=2)
    weighted = weighted * rescale[:, :, None] + jnp.einsum(
        "hqk,khd->hqd", weights.astype(jnp.bfloat16), value_cube, preferred_element_type=jnp.float32
    )
    return (new_max, running_sum, weighted)


def shards(query, key_fresh, value_fresh, key_stale, value_stale, out_weight, residual, gate):
    token_rows = query.shape[0]
    head_count = query.shape[1] // HD
    queries = query.reshape(token_rows, head_count, HD)
    own_start = lax.axis_index("patch") * token_rows
    empty_state = (
        jnp.full((head_count, token_rows), -jnp.inf, jnp.float32),
        jnp.zeros((head_count, token_rows), jnp.float32),
        jnp.zeros((head_count, token_rows, HD), jnp.float32),
    )
    gathered = (
        lax.all_gather(key_stale, "patch", axis=0, tiled=True),
        lax.all_gather(value_stale, "patch", axis=0, tiled=True),
    )
    all_keys = lax.dynamic_update_slice_in_dim(gathered[0], key_fresh, own_start, 0)
    all_values = lax.dynamic_update_slice_in_dim(gathered[1], value_fresh, own_start, 0)
    total_rows = all_keys.shape[0]
    block_size = key_block(total_rows)

    def outer_step(outer_state, block_index):
        offset = block_index * block_size
        block_keys = lax.dynamic_slice_in_dim(all_keys, offset, block_size, 0)
        block_values = lax.dynamic_slice_in_dim(all_values, offset, block_size, 0)
        return (absorb(outer_state, queries, block_keys, block_values), None)

    scanned = lax.scan(
        outer_step, empty_state, jnp.arange(total_rows // block_size, dtype=jnp.int32)
    )
    carried = scanned[0]
    running_max, running_sum, weighted = carried
    mixture = weighted / running_sum[:, :, None]
    attended = (
        jnp.transpose(mixture, (1, 0, 2)).reshape(token_rows, head_count * HD).astype(jnp.bfloat16)
    )
    partial_out = jnp.dot(attended, out_weight, preferred_element_type=jnp.float32)
    summed = lax.psum_scatter(
        partial_out.astype(jnp.bfloat16), "head", scatter_dimension=1, tiled=True
    ).astype(jnp.float32)
    return (residual.astype(jnp.float32) + gate.astype(jnp.float32)[None, :] * summed).astype(
        jnp.bfloat16
    )


def solution(mesh):
    return jax.shard_map(
        shards,
        mesh=mesh,
        in_specs=(
            P("patch", "head"),
            P("patch", "head"),
            P("patch", "head"),
            P("patch", "head"),
            P("patch", "head"),
            P("head", None),
            P("patch", "head"),
            P("head"),
        ),
        out_specs=P("patch", "head"),
        check_vma=False,
    )
```

profile of v0, /device:TPU:1, one launch (start us, length us, event | category | flops | bytes accessed | tf_op | source)
XLA Modules:
  0.0 890.7 jit_solution(12029780691814542948)
XLA Ops:
  9.4 292.8 %all-gather.5.cloned.1.call-done = bf16[12288,640]{1,0:T(8,128)(2,1)} async-done(((bf16[192,640]{1,0:T(8,128)(2,1)}), bf16[12288,640]{1,0:T(8,128)(2,1)}) %all-gather.5.cloned.1.call-update) | async-done | bytes 15728656 | tf_op jit(solution)/shard_map/all_gather | solution.py:47
  303.9 327.4 %all-gather.3.cloned.1.call-done = bf16[12288,640]{1,0:T(8,128)(2,1)} async-done(((bf16[192,640]{1,0:T(8,128)(2,1)}), bf16[12288,640]{1,0:T(8,128)(2,1)}) %all-gather.3.cloned.1.call-update) | async-done | bytes 15728656 | tf_op jit(solution)/shard_map/all_gather | solution.py:46
  632.9 162.1 %while.15 = (s32[]{:T(128)}, f32[5,192]{1,0:T(8,128)S(1)}, f32[5,192]{1,0:T(8,128)S(1)}, f32[5,192,128]{2,1,0:T(8,128)S(1)}, s32[6]{0:T(128)S(1)}, /*index=5*/bf...) while((s32[]{:T(128)}, f32[5,192]{1,0:T(8,128)S(1)}, ...), condition=%wide.region_3.4_spmd.clone, body=%wide.region_0.3_spmd.clone.sunk | while | flops 1022735040 | bytes 61583576 | solution.py:60
  634.2 5.3 constant_dynamic-slice_fusion.3
  642.5 4.3 bitcast_reduce_fusion.2
  646.9 4.8 fusion.29
  654.4 5.5 fusion.31
  661.3 5.3 constant_dynamic-slice_fusion.3
  673.9 4.8 fusion.29
  681.4 5.5 fusion.31
  688.3 5.3 constant_dynamic-slice_fusion.3
  700.9 4.8 fusion.29
  708.5 5.5 fusion.31
  715.3 5.3 constant_dynamic-slice_fusion.3
  727.9 4.8 fusion.29
  735.5 5.5 fusion.31
  742.3 5.3 constant_dynamic-slice_fusion.3
  754.9 4.8 fusion.29
  762.5 5.5 fusion.31
  769.4 5.3 constant_dynamic-slice_fusion.3
  782.0 4.8 fusion.29
  789.5 5.5 fusion.31
  795.5 5.9 convolution_convert_fusion
  801.4 80.8 %reduce-scatter.2.cloned.1.call-done = bf16[192,1280]{1,0:T(8,128)(2,1)} async-done(((bf16[192,5120]{1,0:T(8,128)(2,1)}), bf16[192,1280]{1,0:T(8,128)(2,1)}) %reduce-scatter.2.cloned.1.call-update) | async-done | bytes 491536 | tf_op jit(solution)/shard_map/reduce_scatter | solution.py:70
  (75 shorter events, 68.5 us)
Async XLA Ops:
  6.5 295.7 %all-gather.5.cloned.1.call-start = ((), (), s32[]{:S(2)}) async-start(), calls=%async_computation.2 | async-start | bytes 15974400 | tf_op jit(solution)/shard_map/all_gather | solution.py:47
  7.3 624.0 %all-gather.3.cloned.1.call-start = ((), (), s32[]{:S(2)}) async-start(), calls=%async_computation.1 | async-start | bytes 15974400 | tf_op jit(solution)/shard_map/all_gather | solution.py:46
  8.0 874.3 %reduce-scatter.2.cloned.1.call-start = ((), (), s32[]{:S(2)}) async-start(), calls=%async_computation.3 | async-start | bytes 2457600 | tf_op jit(solution)/shard_map/reduce_scatter | solution.py:70
  646.8 4.8 copy-start
  673.9 4.8 copy-start
  700.9 4.8 copy-start
  727.9 4.8 copy-start
  754.9 4.8 copy-start
  782.0 4.8 copy-start
  795.3 6.1 copy-start.2
  795.3 87.0 %copy-start.1 = (bf16[192,1280]{1,0:T(8,128)(2,1)S(1)}, bf16[192,1280]{1,0:T(8,128)(2,1)}, u32[]{:S(2)}) copy-start(bf16[192,1280]{1,0:T(8,128)(2,1)} %param.16) | copy-start | bytes 1474564
Sparse Core Ops, SparseCore 0:
  9.1 293.0 all-gather.4
  304.0 327.2 all-gather.2
  801.5 80.6 reduce-scatter.1
where the time goes:
time: 891 us
  waiting for transfers between devices  702 us (79%)
  local copies, waits for them, and re-layouts  74.7 us (8%)
  matrix products  64.8 us (7%)
  other arithmetic  31.1 us (3%)
  between operations  13.2 us (1%)
    all_gather x1, waiting for transfers between devices, shards(): lax.all_gather(key_stale, 'patch', axis=0, tiled=True)  327 us
    all_gather x1, waiting for transfers between devices, shards(): lax.all_gather(value_stale, 'patch', axis=0, tiled=True)  293 us
    reduce_scatter x1, waiting for transfers between devices, shards(): lax.psum_scatter(partial_out.astype(jnp.bfloat16), 'head', scatter_dimens...  80.8 us
    dynamic_slice x12, local copies, waits for them, and re-layouts, outer_step(): block_values = lax.dynamic_slice_in_dim(all_values, offset, block_size, 0)  48 us
    dot_general x6, matrix products, absorb(): jnp.einsum('hqk,khd->hqd', weights.astype(jnp.bfloat16), value_cube, pref...  32.9 us
    reduce_sum x6, other arithmetic, absorb(): running_sum = running_sum * rescale + jnp.sum(weights, axis=2)  28.8 us
    dot_general x6, matrix products, absorb(): jnp.einsum('qhd,khd->hqk', queries, key_cube, preferred_element_type=jnp....  26 us
    dynamic_slice x6, local copies, waits for them, and re-layouts, outer_step(): block_keys = lax.dynamic_slice_in_dim(all_keys, offset, block_size, 0)  17.9 us
  transfers between devices with their start and end apart: 3, of which 3 were waited for; matrix products, arithmetic and copies ran while one was open for 0% of the time, Pallas kernels for 0%

commit v1 on v0

v1 whole, which is shorter than its diff:
```python
import functools
import math

import jax
import jax.numpy as jnp
from jax import lax
from jax.experimental import pallas as pl
from jax.experimental.pallas import tpu as pltpu
from jax.sharding import Mesh, PartitionSpec as P

HD = 128
EXP2_SCALE = HD ** (-0.5) * math.log2(math.e)
NY, NX, NZ = 4, 2, 8
GROUP = NY * NX
STAT_ROWS = 16


def attend_kernel(tiles, z_ref, *refs):
    query_refs = refs[:GROUP]
    k_ref, v_ref, fresh_k_ref, fresh_v_ref = refs[GROUP : GROUP + 4]
    out_refs = refs[GROUP + 4 : 2 * GROUP + 4]
    q_buf, k_buf, v_buf, o_buf, lse_buf = refs[2 * GROUP + 4 :]
    rows = query_refs[0].shape[0]
    key_rows = k_ref.shape[0]
    for slot in range(GROUP):
        q_buf[slot * rows : (slot + 1) * rows, :] = query_refs[(slot + 1) % GROUP][...]
    k_buf[...] = k_ref[...]
    v_buf[:, :HD] = v_ref[...]
    v_buf[:, HD:] = jnp.ones((key_rows, HD), jnp.bfloat16)

    def tile(first, count):
        scores = lax.dot_general(
            q_buf[first : first + count, :],
            k_buf[...],
            (((1,), (1,)), ((), ())),
            preferred_element_type=jnp.float32,
        )
        top = jnp.max(scores, axis=1, keepdims=True)
        weights = jnp.exp2((scores - top) * EXP2_SCALE).astype(jnp.bfloat16)
        mixed = jnp.dot(weights, v_buf[...], preferred_element_type=jnp.float32)
        row_sum = mixed[:, HD:]
        o_buf[first : first + count, :] = (mixed[:, :HD] / row_sum).astype(jnp.bfloat16)
        lse_buf[first : first + count, :] = top * EXP2_SCALE + jnp.log2(row_sum)

    first = 0
    for count in tiles:
        tile(first, count)
        first += count
    own = pl.ds(pl.multiple_of(z_ref[0] * rows, rows), rows)
    k_buf[own, :] = fresh_k_ref[...]
    v_buf[own, :HD] = fresh_v_ref[...]
    tile(first, rows)
    for slot in range(GROUP):
        out_ref = out_refs[(slot + 1) % GROUP]
        out_ref[:rows, :] = o_buf[slot * rows : (slot + 1) * rows, :]
        left = jnp.transpose(lse_buf[slot * rows : (slot + 1) * rows, :])[:1, :]
        stat = []
        for _ in range(3):
            part = left.astype(jnp.bfloat16).astype(jnp.float32)
            left = left - part
            stat += [part[:, :HD], jnp.concatenate([part[:, HD:], part[:, HD:]], axis=1)]
        stat.append(jnp.zeros((STAT_ROWS - 6, HD), jnp.float32))
        out_ref[rows:, :] = jnp.concatenate(stat, axis=0).astype(jnp.bfloat16)


def attend(z_index, queries, keys_values, fresh, heads):
    rows = queries[0].shape[0]
    key_rows = keys_values.shape[0]
    q_spec = pl.BlockSpec((rows, HD), lambda h: (0, h))
    return pl.pallas_call(
        functools.partial(attend_kernel, (448, 448, 448)),
        grid=(heads,),
        in_specs=[pl.BlockSpec(memory_space=pltpu.SMEM)]
        + [q_spec] * GROUP
        + [
            pl.BlockSpec((key_rows, HD), lambda h: (0, h)),
            pl.BlockSpec((key_rows, HD), lambda h: (0, h + heads)),
            pl.BlockSpec((rows, HD), lambda h: (0, h)),
            pl.BlockSpec((rows, HD), lambda h: (0, h + heads)),
        ],
        out_specs=[pl.BlockSpec((rows + STAT_ROWS, HD), lambda h: (0, h))] * GROUP,
        out_shape=[jax.ShapeDtypeStruct((rows + STAT_ROWS, heads * HD), jnp.bfloat16)] * GROUP,
        scratch_shapes=[
            pltpu.VMEM((GROUP * rows, HD), jnp.bfloat16),
            pltpu.VMEM((key_rows, HD), jnp.bfloat16),
            pltpu.VMEM((key_rows, 2 * HD), jnp.bfloat16),
            pltpu.VMEM((GROUP * rows, HD), jnp.bfloat16),
            pltpu.VMEM((GROUP * rows, HD), jnp.float32),
        ],
        compiler_params=pltpu.CompilerParams(vmem_limit_bytes=48 * 2**20),
        name="attend",
    )(z_index, *queries, keys_values, keys_values, fresh, fresh)


def combine_kernel(*refs):
    part_refs, out_ref = refs[:GROUP], refs[GROUP]
    rows, width = out_ref.shape
    heads = width // HD
    shares = []
    for head in range(heads):
        columns = slice(head * HD, (head + 1) * HD)
        lse = []
        for ref in part_refs:
            stat = ref[rows:, columns].astype(jnp.float32)
            first = stat[0:1] + stat[2:3] + stat[4:5]
            second = stat[1:2] + stat[3:4] + stat[5:6]
            lse.append(jnp.concatenate([first, second[:, : rows - HD]], axis=1))
        lse = jnp.concatenate(lse, axis=0)
        share = jnp.exp2(lse - jnp.max(lse, axis=0, keepdims=True))
        shares.append(share / jnp.sum(share, axis=0, keepdims=True))
    shares.append(jnp.zeros((HD - heads * GROUP, rows), jnp.float32))
    by_row = jnp.transpose(jnp.concatenate(shares, axis=0))
    for head in range(heads):
        columns = slice(head * HD, (head + 1) * HD)
        total = jnp.zeros((rows, HD), jnp.float32)
        for slot, ref in enumerate(part_refs):
            at = head * GROUP + slot
            total = total + by_row[:, at : at + 1] * ref[:rows, columns].astype(jnp.float32)
        out_ref[:, columns] = total.astype(jnp.bfloat16)


def combine(parts):
    rows, width = parts[0].shape
    return pl.pallas_call(
        combine_kernel,
        out_shape=jax.ShapeDtypeStruct((rows - STAT_ROWS, width), jnp.bfloat16),
        compiler_params=pltpu.CompilerParams(vmem_limit_bytes=32 * 2**20),
        name="combine",
    )(*parts)


def move_yx(array, dy, dx):
    pairs = [
        (y * NX + x, ((y + dy) % NY) * NX + (x + dx) % NX) for y in range(NY) for x in range(NX)
    ]
    return lax.ppermute(array, ("y", "x_lo"), pairs)


OFFSETS = [(dy, dx) for dy in range(NY) for dx in range(NX)]


def shards(query, key_fresh, value_fresh, key_stale, value_stale, out_weight, residual, gate):
    width = query.shape[1]
    heads = width // HD
    columns = residual.shape[1]
    x_hi, core = lax.axis_index("x_hi"), lax.axis_index("core")
    z_index = lax.axis_index("z").astype(jnp.int32).reshape(1)
    keys_values = lax.all_gather(
        jnp.concatenate([key_stale, value_stale], axis=1), "z", axis=0, tiled=True
    )
    fresh = jnp.concatenate([key_fresh, value_fresh], axis=1)
    queries = [query] + [move_yx(query, dy, dx) for dy, dx in OFFSETS[1:]]

    def weight_columns(x_half, core_half):
        return lax.dynamic_slice_in_dim(out_weight, (x_half * 2 + core_half) * columns, columns, 1)

    swap = [(0, 1), (1, 0)]
    sibling_weight = lax.ppermute(
        jnp.stack([weight_columns(1 - x_hi, 1 - core), weight_columns(x_hi, 1 - core)]),
        "core",
        swap,
    )
    own_weight = [weight_columns(1 - x_hi, core), weight_columns(x_hi, core)]

    partials = attend(z_index, queries, keys_values, fresh, heads)
    returned = [partials[0]] + [
        move_yx(part, -dy, -dx) for part, (dy, dx) in zip(partials[1:], OFFSETS[1:])
    ]
    attended = combine(returned)
    sibling = lax.ppermute(attended, "core", swap)

    def project(half):
        return jnp.dot(
            attended, own_weight[half], preferred_element_type=jnp.float32
        ) + jnp.dot(sibling, sibling_weight[half], preferred_element_type=jnp.float32)

    received = lax.ppermute(project(0).astype(jnp.bfloat16), "x_hi", swap)
    projected = project(1) + received.astype(jnp.float32)
    return (
        residual.astype(jnp.float32) + gate.astype(jnp.float32)[None, :] * projected
    ).astype(jnp.bfloat16)


def solution(mesh):
    axes = ("y", "x_lo", "z", "x_hi", "core")
    fine = Mesh(mesh.devices.reshape(NY, NX, NZ, 2, 2), axes)
    rows, cols = ("y", "x_lo", "z"), ("x_hi", "core")
    return jax.shard_map(
        shards,
        mesh=fine,
        in_specs=(
            P(rows, cols),
            P(rows, cols),
            P(rows, cols),
            P(rows, cols),
            P(rows, cols),
            P(cols, None),
            P(rows, cols),
            P(cols),
        ),
        out_specs=P(rows, cols),
        check_vma=False,
    )
```

time: 891 us -> 154 us (0.17)
  waiting for transfers between devices: 702 us -> 65.6 us
  local copies, waits for them, and re-layouts: 74.7 us -> 2.18 us
  matrix products: 64.8 us -> 8.83 us
  starting transfers between devices: 0.08 us -> 38.6 us
  other arithmetic: 31.1 us -> 3.93 us
  Pallas kernels: 0 us -> 20.8 us
    all_gather x2 -> x1, waiting for transfers between devices: 620 us -> 22.1 us  [shards(): lax.all_gather(jnp.concatenate([key_stale, value_stale], axis=1), 'z', ax...]
    reduce_scatter x1 -> x0, waiting for transfers between devices: 80.8 us -> none  [shards(): lax.psum_scatter(partial_out.astype(jnp.bfloat16), 'head', scatter_dimens...]
    dynamic_slice x24 -> x0, local copies, waits for them, and re-layouts: 69.9 us -> none  [the longest x12 48 us: outer_step(): block_values = lax.dynamic_slice_in_dim(all_values, offset, block_size, 0)]
    dot_general x13 -> x4, matrix products: 64.8 us -> 8.83 us  [the longest x2 4.86 us: project(): jnp.dot(attended, own_weight[half], preferred_element_type=jnp.float32)]
    ppermute x0 -> x17, waiting for transfers between devices: none -> 43.5 us  [the longest x14 32.9 us: move_yx(): return lax.ppermute(array, ('y', 'x_lo'), pairs)]
    ppermute x0 -> x17, starting transfers between devices: none -> 38.6 us  [the longest x14 25.6 us: move_yx(): return lax.ppermute(array, ('y', 'x_lo'), pairs)]
    reduce_sum x6 -> x0, other arithmetic: 28.8 us -> none  [absorb(): running_sum = running_sum * rescale + jnp.sum(weights, axis=2)]
    pallas_call x0 -> x2, Pallas kernels: none -> 20.8 us  [the longest x1 19.4 us: attend(): pl.pallas_call(functools.partial(attend_kernel, (448, 448, 448)), grid=(h...]
  transfers between devices with their start and end apart: 3 -> 18, of which waited for: 3 -> 10; matrix products, arithmetic and copies ran while one was open for 0% -> 4% of each run, Pallas kernels for 0% -> 14%
where the time goes in v1:
time: 154 us
  waiting for transfers between devices  65.6 us (43%)
  starting transfers between devices  38.6 us (25%)
  Pallas kernels  20.8 us (14%)
  between operations  13.5 us (9%)
  matrix products  8.83 us (6%)
  other arithmetic  3.93 us (3%)
  local copies, waits for them, and re-layouts  2.18 us (1%)
    ppermute x14, waiting for transfers between devices, move_yx(): return lax.ppermute(array, ('y', 'x_lo'), pairs)  32.9 us
    ppermute x14, starting transfers between devices, move_yx(): return lax.ppermute(array, ('y', 'x_lo'), pairs)  25.6 us
    all_gather x1, waiting for transfers between devices, shards(): lax.all_gather(jnp.concatenate([key_stale, value_stale], axis=1), 'z', ax...  22.1 us
    pallas_call x1, Pallas kernels, attend(): pl.pallas_call(functools.partial(attend_kernel, (448, 448, 448)), grid=(h...  19.4 us
    ppermute x1, waiting for transfers between devices, shards(): received = lax.ppermute(project(0).astype(jnp.bfloat16), 'x_hi', swap)  9.53 us
    ppermute x1, starting transfers between devices, shards(): sibling = lax.ppermute(attended, 'core', swap)  7.26 us
    dot_general x2, matrix products, project(): jnp.dot(attended, own_weight[half], preferred_element_type=jnp.float32)  4.86 us
    dot_general x2, matrix products, project(): jnp.dot(sibling, sibling_weight[half], preferred_element_type=jnp.float32)  3.97 us
  transfers between devices with their start and end apart: 18, of which 10 were waited for; matrix products, arithmetic and copies ran while one was open for 4% of the time, Pallas kernels for 14%

profile of v1, /device:TPU:1, one launch (start us, length us, event | category | flops | bytes accessed | tf_op | source)
XLA Modules:
  0.0 153.6 jit_solution(9185763785018002022)
XLA Ops:
  6.5 1.9 %pad_maximum_fusion.1 = bf16[192,1280]{1,0:T(8,128)(2,1)} fusion(bf16[192,640]{1,0:T(8,128)(2,1)} %param.12, bf16[192,640]{1,0:T(8,128)(2,1)} %param.11), kind=kLoop, calls=%fused_computation.16 | loop fusion | flops 983040 | bytes 983040 | tf_op jit(solution)/shard_map/concatenate | solution.py:149
  8.5 2.1 %dynamic-slice_bitcast_fusion.1 = (bf16[1,640,1280]{2,1,0:T(8,128)(2,1)S(1)}, bf16[1,640,1280]{2,1,0:T(8,128)(2,1)S(1)}) fusion(bf16[640,5120]{1,0:T(8,128)(2,1)} %param.13, s32[]{:T(128)S(6)} %select_n.13, s32[]{:T(128)S(6)} %select_n.14), kind=kLoop, calls=%fused_computation.14 | loop fusion | bytes 6553608 | tf_op jit(solution)/shard_map/stack | solution.py:159
  10.6 2.0 %pad_maximum_fusion = bf16[2,640,1280]{2,1,0:T(8,128)(2,1)} fusion(bf16[1,640,1280]{2,1,0:T(8,128)(2,1)S(1)} %get-tuple-element.22, bf16[1,640,1280]{2,1,0:T(8,128)(2,1)S(1)} %get-tuple-element.21), kind=kLoop, calls=%fused_computation | loop fusion | flops 1638400 | bytes 6553600 | tf_op jit(solution)/shard_map/stack | solution.py:159
  12.7 3.2 %collective-permute-start.15 = (bf16[2,640,1280]{2,1,0:T(8,128)(2,1)}, bf16[2,640,1280]{2,1,0:T(8,128)(2,1)}, u32[]{:S(2)}, u32[]{:S(2)}) collective-permute-start(bf16[2,640,1280]{2,1,0:T(8,128)(2,1)} %pad_maximum_fusion), channel_id=1, source_target_pairs={{0,1},{1,0},{2,3},{3,2},{4,5},{5,4},{6,7},{7,6},{8,9},{9,8},{10,11... | collective-permute-start | bytes 9830408 | tf_op jit(solution)/shard_map/ppermute | solution.py:158
  17.9 3.0 %collective-permute-start.3 = (bf16[192,640]{1,0:T(8,128)(2,1)S(1)}, bf16[192,640]{1,0:T(8,128)(2,1)S(1)}, u32[]{:S(2)}, u32[]{:S(2)}) collective-permute-start(bf16[192,640]{1,0:T(8,128)(2,1)S(1)} %copy-done), channel_id=1, source_target_pairs={{0,128},{32,160},{64,192},{96,224},{128,0},{160,32},{192,64},{224,... | collective-permute-start | bytes 737288 | tf_op jit(solution)/shard_map/ppermute | solution.py:136
  20.9 2.5 %collective-permute-done.refs_1_ = bf16[192,640]{1,0:T(8,128)(2,1)S(1)} collective-permute-done((bf16[192,640]{1,0:T(8,128)(2,1)S(1)}, bf16[192,640]{1,0:T(8,128)(2,1)S(1)}, u32[]{:S(2)}, u32[]{:S(2)}) %collective-permute-start) | collective-permute-done | bytes 245792 | tf_op jit(solution)/shard_map/ppermute | solution.py:136
  23.5 2.1 %collective-permute-start.4 = (bf16[192,640]{1,0:T(8,128)(2,1)S(1)}, bf16[192,640]{1,0:T(8,128)(2,1)S(1)}, u32[]{:S(2)}, u32[]{:S(2)}) collective-permute-start(bf16[192,640]{1,0:T(8,128)(2,1)S(1)} %copy-done), channel_id=1, source_target_pairs={{0,160},{32,128},{64,224},{96,192},{128,32},{160,0},{192,96},{224,... | collective-permute-start | bytes 737288 | tf_op jit(solution)/shard_map/ppermute | solution.py:136
  25.6 10.3 %collective-permute-start.5 = (bf16[192,640]{1,0:T(8,128)(2,1)S(1)}, bf16[192,640]{1,0:T(8,128)(2,1)S(1)}, u32[]{:S(2)}, u32[]{:S(2)}) collective-permute-start(bf16[192,640]{1,0:T(8,128)(2,1)S(1)} %copy-done), channel_id=1, source_target_pairs={{0,192},{32,224},{64,0},{96,32},{128,64},{160,96},{192,128},{224,1... | collective-permute-start | bytes 737288 | tf_op jit(solution)/shard_map/ppermute | solution.py:136
  36.0 4.9 %collective-permute-done.3.refs_4_ = bf16[192,640]{1,0:T(8,128)(2,1)S(1)} collective-permute-done((bf16[192,640]{1,0:T(8,128)(2,1)S(1)}, bf16[192,640]{1,0:T(8,128)(2,1)S(1)}, u32[]{:S(2)}, u32[]{:S(2)}) %collective-permute-start.3) | collective-permute-done | bytes 245792 | tf_op jit(solution)/shard_map/ppermute | solution.py:136
  40.9 2.3 %collective-permute-done.5.refs_6_ = bf16[192,640]{1,0:T(8,128)(2,1)S(1)} collective-permute-done((bf16[192,640]{1,0:T(8,128)(2,1)S(1)}, bf16[192,640]{1,0:T(8,128)(2,1)S(1)}, u32[]{:S(2)}, u32[]{:S(2)}) %collective-permute-start.5) | collective-permute-done | bytes 245792 | tf_op jit(solution)/shard_map/ppermute | solution.py:136
  43.2 22.1 %all-gather.2.cloned.1.call-done.refs_8_.refs_9_ = bf16[1536,1280]{1,0:T(8,128)(2,1)} async-done(((bf16[192,1280]{1,0:T(8,128)(2,1)}), bf16[1536,1280]{1,0:T(8,128)(2,1)}) %all-gather.2.cloned.1.call-update) | async-done | bytes 3932176 | tf_op jit(solution)/shard_map/all_gather | solution.py:148
  65.3 19.4 %attend.1 = (bf16[208,640]{1,0:T(8,128)(2,1)S(1)}, bf16[208,640]{1,0:T(8,128)(2,1)S(1)}, bf16[208,640]{1,0:T(8,128)(2,1)S(1)}, bf16[208,640]{1,0:T(8,128)(2,1)S(...) custom-call(s32[1]{0:T(128)} %bitcast.z_ref, ...), custom_call_target="tpu_custom_call" | custom-call | tf_op jit(solution)/shard_map/attend/pallas_call | solution.py:70
  86.1 2.5 %collective-permute-start.8 = (bf16[208,640]{1,0:T(8,128)(2,1)S(1)}, bf16[208,640]{1,0:T(8,128)(2,1)S(1)}, u32[]{:S(2)}, u32[]{:S(2)}) collective-permute-start(bf16[208,640]{1,0:T(8,128)(2,1)S(1)} %get-tuple-element.15), channel_id=1, source_target_pairs={{0,192},{32,224},{64,0},{96,32},{128,64},{160,96},{192,128},{224,1... | collective-permute-start | bytes 798728 | tf_op jit(solution)/shard_map/ppermute | solution.py:136
  89.3 2.8 %collective-permute-done.7.refs_1_ = bf16[208,640]{1,0:T(8,128)(2,1)S(1)} collective-permute-done((bf16[208,640]{1,0:T(8,128)(2,1)S(1)}, bf16[208,640]{1,0:T(8,128)(2,1)S(1)}, u32[]{:S(2)}, u32[]{:S(2)}) %collective-permute-start.7) | collective-permute-done | bytes 266272 | tf_op jit(solution)/shard_map/ppermute | solution.py:136
  92.1 3.6 %collective-permute-start.11 = (bf16[208,640]{1,0:T(8,128)(2,1)S(1)}, bf16[208,640]{1,0:T(8,128)(2,1)S(1)}, u32[]{:S(2)}, u32[]{:S(2)}) collective-permute-start(bf16[208,640]{1,0:T(8,128)(2,1)S(1)} %get-tuple-element.18), channel_id=1, source_target_pairs={{0,160},{32,128},{64,224},{96,192},{128,32},{160,0},{192,96},{224,... | collective-permute-start | bytes 798728 | tf_op jit(solution)/shard_map/ppermute | solution.py:136
  95.8 9.7 %collective-permute-done.8.refs_2_ = bf16[208,640]{1,0:T(8,128)(2,1)S(1)} collective-permute-done((bf16[208,640]{1,0:T(8,128)(2,1)S(1)}, bf16[208,640]{1,0:T(8,128)(2,1)S(1)}, u32[]{:S(2)}, u32[]{:S(2)}) %collective-permute-start.8) | collective-permute-done | bytes 266272 | tf_op jit(solution)/shard_map/ppermute | solution.py:136
  106.2 9.8 %collective-permute-done.12.refs_6_ = bf16[208,640]{1,0:T(8,128)(2,1)S(1)} collective-permute-done((bf16[208,640]{1,0:T(8,128)(2,1)S(1)}, bf16[208,640]{1,0:T(8,128)(2,1)S(1)}, u32[]{:S(2)}, u32[]{:S(2)}) %collective-permute-start.12) | collective-permute-done | bytes 266272 | tf_op jit(solution)/shard_map/ppermute | solution.py:136
  117.4 7.3 %collective-permute-start.14 = (bf16[192,640]{1,0:T(8,128)(2,1)S(1)}, bf16[192,640]{1,0:T(8,128)(2,1)S(1)}, u32[]{:S(2)}, u32[]{:S(2)}) collective-permute-start(bf16[192,640]{1,0:T(8,128)(2,1)S(1)} %combine.1), channel_id=1, source_target_pairs={{0,1},{1,0},{2,3},{3,2},{4,5},{5,4},{6,7},{7,6},{8,9},{9,8},{10,11... | collective-permute-start | bytes 737288 | tf_op jit(solution)/shard_map/ppermute | solution.py:170
  125.8 2.0 %fusion.5 = f32[192,1280]{1,0:T(8,128)S(1)} fusion(bf16[192,640]{1,0:T(8,128)(2,1)S(1)} %collective-permute-done.14, bf16[2,640,1280]{2,1,0:T(8,128)(2,1)} %collective-permute-done.15), kind=kOutput, calls=%fused_computation.9 | convolution fusion | flops 314572800 | bytes 2867200 | tf_op jit(solution)/shard_map/dot_general | solution.py:175
  127.8 2.0 %fusion.3 = bf16[192,1280]{1,0:T(8,128)(2,1)S(1)} fusion(f32[192,1280]{1,0:T(8,128)S(1)} %fusion.5, bf16[192,640]{1,0:T(8,128)(2,1)S(1)} %combine.1, bf16[640,5120]{1,0:T(8,128)(2,1)} %param.13, s32[]{:T(128)S(6)} %select_n.15), kind=kOutput, calls=%fused_computation.6 | convolution fusion | flops 315064320 | bytes 3358724 | tf_op jit(solution)/shard_map/dot_general | solution.py:173
  129.9 2.5 %collective-permute-start.16 = (bf16[192,1280]{1,0:T(8,128)(2,1)S(1)}, bf16[192,1280]{1,0:T(8,128)(2,1)S(1)}, u32[]{:S(2)}, u32[]{:S(2)}) collective-permute-start(bf16[192,1280]{1,0:T(8,128)(2,1)S(1)} %fusion.3), channel_id=1, source_target_pairs={{0,2},{2,0},{1,3},{3,1},{4,6},{6,4},{5,7},{7,5},{8,10},{10,8},{9,1... | collective-permute-start | bytes 1474568 | tf_op jit(solution)/shard_map/ppermute | solution.py:177
  132.4 2.0 %fusion.6 = f32[192,1280]{1,0:T(8,128)S(1)} fusion(bf16[192,640]{1,0:T(8,128)(2,1)S(1)} %collective-permute-done.14, bf16[2,640,1280]{2,1,0:T(8,128)(2,1)} %collective-permute-done.15), kind=kOutput, calls=%fused_computation.11 | convolution fusion | flops 314572800 | bytes 2867200 | tf_op jit(solution)/shard_map/dot_general | solution.py:175
  134.4 9.5 %collective-permute-done.16 = bf16[192,1280]{1,0:T(8,128)(2,1)S(1)} collective-permute-done((bf16[192,1280]{1,0:T(8,128)(2,1)S(1)}, bf16[192,1280]{1,0:T(8,128)(2,1)S(1)}, u32[]{:S(2)}, u32[]{:S(2)}) %collective-permute-start.16) | collective-permute-done | bytes 491552 | tf_op jit(solution)/shard_map/ppermute | solution.py:177
  143.9 2.8 %fusion.4 = bf16[192,1280]{1,0:T(8,128)(2,1)} fusion(f32[192,1280]{1,0:T(8,128)S(1)} %fusion.6, bf16[192,640]{1,0:T(8,128)(2,1)S(1)} %combine.1, bf16[640,5120]{1,0:T(8,128)(2,1)} %param.13, s32[]{:T(128)S(6)} %select_n.12, bf16[192,1280]{1,0:T(8,128)(2,1)S(1)} %collective-permute-done.16, bf16[192,1280]{1,0:T(8,128)(2,1)S(1)} %copy-done.1, ...), kind=kOutput, calls=%fused_computation.7 | convolution fusion | flops 316293120 | bytes 4346884 | tf_op jit(solution)/shard_map/dot_general | solution.py:173
  (34 shorter events, 7.5 us)
Async XLA Ops:
  6.5 58.8 %all-gather.2.cloned.1.call-start = ((), (), s32[]{:S(2)}) async-start(), calls=%async_computation | async-start | bytes 4423680 | tf_op jit(solution)/shard_map/all_gather | solution.py:148
  10.6 5.3 %copy-start = (bf16[192,640]{1,0:T(8,128)(2,1)S(1)}, bf16[192,640]{1,0:T(8,128)(2,1)}, u32[]{:S(2)}) copy-start(bf16[192,640]{1,0:T(8,128)(2,1)} %refs_0_.1) | copy-start | bytes 737284
  10.6 25.3 %copy-start.2 = (bf16[192,640]{1,0:T(8,128)(2,1)S(1)}, bf16[192,640]{1,0:T(8,128)(2,1)}, u32[]{:S(2)}) copy-start(bf16[192,640]{1,0:T(8,128)(2,1)} %param.10) | copy-start | bytes 737284
  10.6 25.3 %copy-start.3 = (bf16[192,640]{1,0:T(8,128)(2,1)S(1)}, bf16[192,640]{1,0:T(8,128)(2,1)}, u32[]{:S(2)}) copy-start(bf16[192,640]{1,0:T(8,128)(2,1)} %param.9) | copy-start | bytes 737284
  12.7 112.0 %collective-permute-start.15 = (bf16[2,640,1280]{2,1,0:T(8,128)(2,1)}, bf16[2,640,1280]{2,1,0:T(8,128)(2,1)}, u32[]{:S(2)}, u32[]{:S(2)}) collective-permute-start(bf16[2,640,1280]{2,1,0:T(8,128)(2,1)} %pad_maximum_fusion), channel_id=1, source_target_pairs={{0,1},{1,0},{2,3},{3,2},{4,5},{5,4},{6,7},{7,6},{8,9},{9,8},{10,11... | collective-permute-start | bytes 9830408 | tf_op jit(solution)/shard_map/ppermute | solution.py:158
  15.9 7.6 %collective-permute-start = (bf16[192,640]{1,0:T(8,128)(2,1)S(1)}, bf16[192,640]{1,0:T(8,128)(2,1)S(1)}, u32[]{:S(2)}, u32[]{:S(2)}) collective-permute-start(bf16[192,640]{1,0:T(8,128)(2,1)S(1)} %copy-done), channel_id=1, source_target_pairs={{0,32},{32,0},{64,96},{96,64},{128,160},{160,128},{192,224},{224,1... | collective-permute-start | bytes 737288 | tf_op jit(solution)/shard_map/ppermute | solution.py:136
  15.9 9.7 %collective-permute-start.1 = (bf16[192,640]{1,0:T(8,128)(2,1)S(1)}, bf16[192,640]{1,0:T(8,128)(2,1)S(1)}, u32[]{:S(2)}, u32[]{:S(2)}) collective-permute-start(bf16[192,640]{1,0:T(8,128)(2,1)S(1)} %copy-done), channel_id=1, source_target_pairs={{0,64},{32,96},{64,128},{96,160},{128,192},{160,224},{192,0},{224,... | collective-permute-start | bytes 737288 | tf_op jit(solution)/shard_map/ppermute | solution.py:136
  16.7 19.2 %collective-permute-start.2 = (bf16[192,640]{1,0:T(8,128)(2,1)S(1)}, bf16[192,640]{1,0:T(8,128)(2,1)S(1)}, u32[]{:S(2)}, u32[]{:S(2)}) collective-permute-start(bf16[192,640]{1,0:T(8,128)(2,1)S(1)} %copy-done), channel_id=1, source_target_pairs={{0,96},{32,64},{64,160},{96,128},{128,224},{160,192},{192,32},{224... | collective-permute-start | bytes 737288 | tf_op jit(solution)/shard_map/ppermute | solution.py:136
  17.9 23.0 %collective-permute-start.3 = (bf16[192,640]{1,0:T(8,128)(2,1)S(1)}, bf16[192,640]{1,0:T(8,128)(2,1)S(1)}, u32[]{:S(2)}, u32[]{:S(2)}) collective-permute-start(bf16[192,640]{1,0:T(8,128)(2,1)S(1)} %copy-done), channel_id=1, source_target_pairs={{0,128},{32,160},{64,192},{96,224},{128,0},{160,32},{192,64},{224,... | collective-permute-start | bytes 737288 | tf_op jit(solution)/shard_map/ppermute | solution.py:136
  23.5 17.4 %collective-permute-start.4 = (bf16[192,640]{1,0:T(8,128)(2,1)S(1)}, bf16[192,640]{1,0:T(8,128)(2,1)S(1)}, u32[]{:S(2)}, u32[]{:S(2)}) collective-permute-start(bf16[192,640]{1,0:T(8,128)(2,1)S(1)} %copy-done), channel_id=1, source_target_pairs={{0,160},{32,128},{64,224},{96,192},{128,32},{160,0},{192,96},{224,... | collective-permute-start | bytes 737288 | tf_op jit(solution)/shard_map/ppermute | solution.py:136
  25.6 17.6 %collective-permute-start.5 = (bf16[192,640]{1,0:T(8,128)(2,1)S(1)}, bf16[192,640]{1,0:T(8,128)(2,1)S(1)}, u32[]{:S(2)}, u32[]{:S(2)}) collective-permute-start(bf16[192,640]{1,0:T(8,128)(2,1)S(1)} %copy-done), channel_id=1, source_target_pairs={{0,192},{32,224},{64,0},{96,32},{128,64},{160,96},{192,128},{224,1... | collective-permute-start | bytes 737288 | tf_op jit(solution)/shard_map/ppermute | solution.py:136
  35.9 7.3 %collective-permute-start.6 = (bf16[192,640]{1,0:T(8,128)(2,1)S(1)}, bf16[192,640]{1,0:T(8,128)(2,1)S(1)}, u32[]{:S(2)}, u32[]{:S(2)}) collective-permute-start(bf16[192,640]{1,0:T(8,128)(2,1)S(1)} %copy-done), channel_id=1, source_target_pairs={{0,224},{32,192},{64,32},{96,0},{128,96},{160,64},{192,160},{224,1... | collective-permute-start | bytes 737288 | tf_op jit(solution)/shard_map/ppermute | solution.py:136
  84.8 7.3 %collective-permute-start.7 = (bf16[208,640]{1,0:T(8,128)(2,1)S(1)}, bf16[208,640]{1,0:T(8,128)(2,1)S(1)}, u32[]{:S(2)}, u32[]{:S(2)}) collective-permute-start(bf16[208,640]{1,0:T(8,128)(2,1)S(1)} %get-tuple-element.14), channel_id=1, source_target_pairs={{0,32},{32,0},{64,96},{96,64},{128,160},{160,128},{192,224},{224,1... | collective-permute-start | bytes 798728 | tf_op jit(solution)/shard_map/ppermute | solution.py:136
  86.1 19.4 %collective-permute-start.8 = (bf16[208,640]{1,0:T(8,128)(2,1)S(1)}, bf16[208,640]{1,0:T(8,128)(2,1)S(1)}, u32[]{:S(2)}, u32[]{:S(2)}) collective-permute-start(bf16[208,640]{1,0:T(8,128)(2,1)S(1)} %get-tuple-element.15), channel_id=1, source_target_pairs={{0,192},{32,224},{64,0},{96,32},{128,64},{160,96},{192,128},{224,1... | collective-permute-start | bytes 798728 | tf_op jit(solution)/shard_map/ppermute | solution.py:136
  88.5 16.9 %collective-permute-start.9 = (bf16[208,640]{1,0:T(8,128)(2,1)S(1)}, bf16[208,640]{1,0:T(8,128)(2,1)S(1)}, u32[]{:S(2)}, u32[]{:S(2)}) collective-permute-start(bf16[208,640]{1,0:T(8,128)(2,1)S(1)} %get-tuple-element.16), channel_id=1, source_target_pairs={{0,224},{32,192},{64,32},{96,0},{128,96},{160,64},{192,160},{224,1... | collective-permute-start | bytes 798728 | tf_op jit(solution)/shard_map/ppermute | solution.py:136
  89.1 16.4 %collective-permute-start.10 = (bf16[208,640]{1,0:T(8,128)(2,1)S(1)}, bf16[208,640]{1,0:T(8,128)(2,1)S(1)}, u32[]{:S(2)}, u32[]{:S(2)}) collective-permute-start(bf16[208,640]{1,0:T(8,128)(2,1)S(1)} %get-tuple-element.17), channel_id=1, source_target_pairs={{0,128},{32,160},{64,192},{96,224},{128,0},{160,32},{192,64},{224,... | collective-permute-start | bytes 798728 | tf_op jit(solution)/shard_map/ppermute | solution.py:136
  92.1 14.0 %collective-permute-start.11 = (bf16[208,640]{1,0:T(8,128)(2,1)S(1)}, bf16[208,640]{1,0:T(8,128)(2,1)S(1)}, u32[]{:S(2)}, u32[]{:S(2)}) collective-permute-start(bf16[208,640]{1,0:T(8,128)(2,1)S(1)} %get-tuple-element.18), channel_id=1, source_target_pairs={{0,160},{32,128},{64,224},{96,192},{128,32},{160,0},{192,96},{224,... | collective-permute-start | bytes 798728 | tf_op jit(solution)/shard_map/ppermute | solution.py:136
  105.4 10.6 %collective-permute-start.12 = (bf16[208,640]{1,0:T(8,128)(2,1)S(1)}, bf16[208,640]{1,0:T(8,128)(2,1)S(1)}, u32[]{:S(2)}, u32[]{:S(2)}) collective-permute-start(bf16[208,640]{1,0:T(8,128)(2,1)S(1)} %get-tuple-element.19), channel_id=1, source_target_pairs={{0,64},{32,96},{64,128},{96,160},{128,192},{160,224},{192,0},{224,... | collective-permute-start | bytes 798728 | tf_op jit(solution)/shard_map/ppermute | solution.py:136
  105.5 10.6 %collective-permute-start.13 = (bf16[208,640]{1,0:T(8,128)(2,1)S(1)}, bf16[208,640]{1,0:T(8,128)(2,1)S(1)}, u32[]{:S(2)}, u32[]{:S(2)}) collective-permute-start(bf16[208,640]{1,0:T(8,128)(2,1)S(1)} %get-tuple-element.20), channel_id=1, source_target_pairs={{0,96},{32,64},{64,160},{96,128},{128,224},{160,192},{192,32},{224... | collective-permute-start | bytes 798728 | tf_op jit(solution)/shard_map/ppermute | solution.py:136
  117.4 15.0 %copy-start.4 = (bf16[1280]{0:T(1024)(128)(2,1)S(1)}, bf16[1280]{0:T(1024)(128)(2,1)}, u32[]{:S(2)}) copy-start(bf16[1280]{0:T(1024)(128)(2,1)} %param.15) | copy-start | bytes 7684
  117.4 8.4 %collective-permute-start.14 = (bf16[192,640]{1,0:T(8,128)(2,1)S(1)}, bf16[192,640]{1,0:T(8,128)(2,1)S(1)}, u32[]{:S(2)}, u32[]{:S(2)}) collective-permute-start(bf16[192,640]{1,0:T(8,128)(2,1)S(1)} %combine.1), channel_id=1, source_target_pairs={{0,1},{1,0},{2,3},{3,2},{4,5},{5,4},{6,7},{7,6},{8,9},{9,8},{10,11... | collective-permute-start | bytes 737288 | tf_op jit(solution)/shard_map/ppermute | solution.py:170
  127.8 16.1 %copy-start.1 = (bf16[192,1280]{1,0:T(8,128)(2,1)S(1)}, bf16[192,1280]{1,0:T(8,128)(2,1)}, u32[]{:S(2)}) copy-start(bf16[192,1280]{1,0:T(8,128)(2,1)} %param.14) | copy-start | bytes 1474564
  129.9 14.0 %collective-permute-start.16 = (bf16[192,1280]{1,0:T(8,128)(2,1)S(1)}, bf16[192,1280]{1,0:T(8,128)(2,1)S(1)}, u32[]{:S(2)}, u32[]{:S(2)}) collective-permute-start(bf16[192,1280]{1,0:T(8,128)(2,1)S(1)} %fusion.3), channel_id=1, source_target_pairs={{0,2},{2,0},{1,3},{3,1},{4,6},{6,4},{5,7},{7,5},{8,10},{10,8},{9,1... | collective-permute-start | bytes 1474568 | tf_op jit(solution)/shard_map/ppermute | solution.py:177
Sparse Core Ops, SparseCore 0:
  9.1 56.1 all-gather.1

commit v2 on v0

v2 whole, which is shorter than its diff:
```python
import functools
import math

import jax
import jax.numpy as jnp
from jax import lax
from jax.experimental import pallas as pl
from jax.experimental.pallas import tpu as pltpu
from jax.sharding import Mesh, PartitionSpec as P

HD = 128
EXP2_SCALE = HD ** (-0.5) * math.log2(math.e)
NY, NX, NZ = 4, 2, 8
STAT_ROWS = 16
BIG = 60
OFFSETS = [(dy, dx) for dy in range(NY) for dx in range(NX)]


def pipelined(tile_count, scores_of, finish):
    scores = scores_of(0)
    for index in range(tile_count):
        following = scores_of(index + 1) if index + 1 < tile_count else None
        finish(index, scores)
        scores = following


def multiply_keys(queries, keys):
    return lax.dot_general(
        queries, keys, (((1,), (1,)), ((), ())), preferred_element_type=jnp.float32
    )


def mix(scores, values):
    top = jnp.max(scores, axis=1, keepdims=True)
    weights = jnp.exp2((scores - top) * EXP2_SCALE).astype(jnp.bfloat16)
    mixed = jnp.dot(weights, values, preferred_element_type=jnp.float32)
    return top * EXP2_SCALE, mixed[:, :HD], mixed[:, HD:]


def attention_cost(products):
    return pl.CostEstimate(flops=16 * products, bytes_accessed=0, transcendentals=products // HD)


class Arrivals:
    def __init__(self, sems):
        self.sems, self.copies, self.open = sems, [], []

    def start(self, source, target):
        copy = pltpu.make_async_copy(source, target, self.sems.at[len(self.copies)])
        copy.start()
        self.copies.append(copy)
        self.open.append(True)
        return len(self.copies) - 1

    def wait(self, *names):
        for name in names:
            if self.open[name]:
                self.copies[name].wait()
                self.open[name] = False


def head_columns(head):
    return slice(head * HD, (head + 1) * HD)


def with_ones(values):
    return jnp.concatenate([values, jnp.ones(values.shape, values.dtype)], axis=1)


def stat_rows(column):
    lines = []
    for first in range(0, column.shape[0], HD):
        piece = column[first : first + HD, :]
        on_diagonal = lax.broadcasted_iota(jnp.int32, piece.shape, 0) == lax.broadcasted_iota(
            jnp.int32, piece.shape, 1
        )
        lines.append(jnp.sum(jnp.where(on_diagonal, piece, 0.0), axis=0, keepdims=True))
    left = jnp.concatenate(lines, axis=0)
    stat = []
    for _ in range(3):
        part = left.astype(jnp.bfloat16).astype(jnp.float32)
        left = left - part
        stat.append(part)
    stat.append(jnp.zeros((STAT_ROWS - 6, HD), jnp.float32))
    return jnp.concatenate(stat, axis=0).astype(jnp.bfloat16)


def attend_kernel(groups, blocks, place_ref, query_ref, around_ref, *refs):
    block_refs, refs = refs[:blocks], refs[blocks:]
    k_refs, v_refs = block_refs[::2], block_refs[1::2]
    fresh_k_ref, fresh_v_ref, out_ref, refs = *refs[:3], refs[3:]
    q_buf, k_buf, v_buf, fresh_k, fresh_v, out_buf, sems = refs
    rows, width = query_ref.shape
    heads = width // HD
    arrivals = Arrivals(sems)
    got_q = {}
    y, x = place_ref[0], place_ref[1]

    def lines(slot, count=1):
        return pl.ds(slot * rows, count * rows)

    def source(slot):
        dy, dx = OFFSETS[slot]
        return lax.rem(y + NY - dy, NY), lax.rem(x + NX - dx, NX)

    def fetch(group):
        first, count = group[0], len(group)
        if first:
            dx = OFFSETS[first][1]
            from_ref = around_ref.at[source(first)[0], pl.ds(dx * rows, count * rows)]
        else:
            from_ref = query_ref
        got_q[group] = arrivals.start(from_ref, q_buf.at[lines(first, count)])

    fetch(groups[0])
    got_k = [arrivals.start(ref, k_buf.at[lines(i)]) for i, ref in enumerate(k_refs)]
    got_v = [arrivals.start(ref, v_buf.at[lines(i)]) for i, ref in enumerate(v_refs)]
    for group in groups[1:]:
        fetch(group)
    got_fresh_k = arrivals.start(fresh_k_ref, fresh_k)
    got_fresh_v = arrivals.start(fresh_v_ref, fresh_v)
    tiles = [(group, head) for group in groups for head in range(heads)]

    def scores_of(i):
        group, head = tiles[i]
        columns = head_columns(head)
        arrivals.wait(got_q[group], *got_k)
        keys = k_buf[:, columns]
        if 0 in group:
            arrivals.wait(got_fresh_k)
            keys = jnp.concatenate([fresh_k[:, columns], k_buf[rows:, columns]], axis=0)
        return multiply_keys(q_buf[lines(group[0], len(group)), columns], keys)

    def finish(i, scores):
        group, head = tiles[i]
        columns = head_columns(head)
        arrivals.wait(*got_v)
        values = v_buf[:, columns]
        if 0 in group:
            arrivals.wait(got_fresh_v)
            values = jnp.concatenate([fresh_v[:, columns], v_buf[rows:, columns]], axis=0)
        top, mixed, row_sum = mix(scores, with_ones(values))
        mixture = (mixed / row_sum).astype(jnp.bfloat16)
        lse = top + jnp.log2(row_sum)
        for i, slot in enumerate(group):
            at = slice(i * rows, (i + 1) * rows)
            out_buf[slot, :rows, columns] = mixture[at]
            out_buf[slot, rows:, columns] = stat_rows(lse[at])
            if head == heads - 1:
                to_y, to_x = source(slot)
                arrivals.start(out_buf.at[slot], out_ref.at[to_y * NX + to_x])

    pipelined(len(tiles), scores_of, finish)
    arrivals.wait(*range(len(arrivals.copies)))


def attend(groups, place, query, around, blocks, fresh_key, fresh_value):
    rows, width = query.shape
    slots, count = len(OFFSETS), len(blocks)
    anywhere = pl.BlockSpec(memory_space=pl.ANY)
    return pl.pallas_call(
        functools.partial(attend_kernel, groups, 2 * count),
        in_specs=[pl.BlockSpec(memory_space=pltpu.SMEM)] + [anywhere] * (4 + 2 * count),
        out_specs=anywhere,
        out_shape=jax.ShapeDtypeStruct((slots, rows + STAT_ROWS, width), jnp.bfloat16),
        scratch_shapes=[
            pltpu.VMEM((slots * rows, width), jnp.bfloat16),
            pltpu.VMEM((count * rows, width), jnp.bfloat16),
            pltpu.VMEM((count * rows, width), jnp.bfloat16),
            pltpu.VMEM((rows, width), jnp.bfloat16),
            pltpu.VMEM((rows, width), jnp.bfloat16),
            pltpu.VMEM((slots, rows + STAT_ROWS, width), jnp.bfloat16),
            pltpu.SemaphoreType.DMA((2 * slots + 2 * count + 2,)),
        ],
        compiler_params=pltpu.CompilerParams(vmem_limit_bytes=BIG * 2**20),
        cost_estimate=attention_cost(slots * rows * count * rows * width),
        name="attend",
    )(
        place,
        query,
        around,
        *[array for block in blocks for array in block],
        fresh_key,
        fresh_value,
    )


def repeat_kernel(a_ref, b_ref, out_ref):
    rows = a_ref.shape[0]
    out_ref[:rows, :] = a_ref[...]
    out_ref[rows:, :] = b_ref[...]


def repeat(a, b, times):
    rows, width = a.shape
    whole = pl.BlockSpec((rows, width), lambda i: (0, 0))
    return pl.pallas_call(
        repeat_kernel,
        grid=(times,),
        in_specs=[whole, whole],
        out_specs=pl.BlockSpec((None, 2 * rows, width), lambda i: (i, 0, 0)),
        out_shape=jax.ShapeDtypeStruct((times, 2 * rows, width), a.dtype),
        compiler_params=pltpu.CompilerParams(vmem_limit_bytes=BIG * 2**20),
        name="repeat",
    )(a, b)


def combine_kernel(blocks_ref, parts_ref, w_ref, out_ref, first_ref, second_ref, w_buf, sems):
    product_refs = (first_ref, second_ref)
    columns = first_ref.shape[1]
    copies = []
    for i in range(len(product_refs)):
        first = pl.multiple_of(blocks_ref[i] * columns, columns)
        copy = pltpu.make_async_copy(w_ref.at[:, pl.ds(first, columns)], w_buf.at[i], sems.at[i])
        copy.start()
        copies.append(copy)
    group = parts_ref.shape[0]
    rows, width = out_ref.shape
    heads = width // HD
    shares = []
    for head in range(heads):
        columns = slice(head * HD, (head + 1) * HD)
        lse = []
        for part in range(group):
            stat = parts_ref[part, rows:, columns].astype(jnp.float32)
            lines = stat[0:2] + stat[2:4] + stat[4:6]
            lse.append(jnp.concatenate([lines[:1], lines[1:2, : rows - HD]], axis=1))
        lse = jnp.concatenate(lse, axis=0)
        share = jnp.exp2(lse - jnp.max(lse, axis=0, keepdims=True))
        shares.append(share / jnp.sum(share, axis=0, keepdims=True))
    shares.append(jnp.zeros((HD - heads * group, rows), jnp.float32))
    by_row = jnp.transpose(jnp.concatenate(shares, axis=0))
    for head in range(heads):
        columns = slice(head * HD, (head + 1) * HD)
        total = jnp.zeros((rows, HD), jnp.float32)
        for part in range(group):
            at = head * group + part
            mixture = parts_ref[part, :rows, columns].astype(jnp.float32)
            total = total + by_row[:, at : at + 1] * mixture
        out_ref[:, columns] = total.astype(jnp.bfloat16)
    for i, product_ref in enumerate(product_refs):
        copies[i].wait()
        product_ref[...] = jnp.dot(
            out_ref[...], w_buf[i], preferred_element_type=jnp.float32
        ).astype(jnp.bfloat16)


def combine(blocks, parts, out_weight, columns):
    _, rows, width = parts.shape
    rows -= STAT_ROWS
    vmem = pl.BlockSpec(memory_space=pltpu.VMEM)
    return pl.pallas_call(
        combine_kernel,
        in_specs=[
            pl.BlockSpec(memory_space=pltpu.SMEM),
            vmem,
            pl.BlockSpec(memory_space=pl.ANY),
        ],
        out_specs=[vmem, vmem, vmem],
        out_shape=[
            jax.ShapeDtypeStruct((rows, width), jnp.bfloat16),
            jax.ShapeDtypeStruct((rows, columns), jnp.bfloat16),
            jax.ShapeDtypeStruct((rows, columns), jnp.bfloat16),
        ],
        scratch_shapes=[
            pltpu.VMEM((2, width, columns), jnp.bfloat16),
            pltpu.SemaphoreType.DMA((2,)),
        ],
        compiler_params=pltpu.CompilerParams(vmem_limit_bytes=BIG * 2**20),
        name="combine",
    )(blocks, parts, out_weight)


def project_kernel(block_ref, a_ref, w_ref, out_ref):
    out_ref[...] = jnp.dot(
        a_ref[...], w_ref[...], preferred_element_type=jnp.float32
    ).astype(out_ref.dtype)


def project(block, attended, out_weight, columns, dtype):
    rows, width = attended.shape
    steps = 2
    part = columns // steps
    return pl.pallas_call(
        project_kernel,
        grid_spec=pltpu.PrefetchScalarGridSpec(
            num_scalar_prefetch=1,
            grid=(steps,),
            in_specs=[
                pl.BlockSpec((rows, width), lambda i, block: (0, 0)),
                pl.BlockSpec((width, part), lambda i, block: (0, block[0] * steps + i)),
            ],
            out_specs=pl.BlockSpec((rows, part), lambda i, block: (0, i)),
        ),
        out_shape=jax.ShapeDtypeStruct((rows, columns), dtype),
        compiler_params=pltpu.CompilerParams(vmem_limit_bytes=BIG * 2**20),
        name="project",
    )(block, attended, out_weight)


def move_z(array, step):
    return lax.ppermute(array, "z", [(z, (z + step) % NZ) for z in range(NZ)])


def shards(query, key_fresh, value_fresh, key_stale, value_stale, out_weight, residual, gate):
    columns = residual.shape[1]
    x_hi, core = lax.axis_index("x_hi"), lax.axis_index("core")

    swap = [(0, 1), (1, 0)]
    stacked = repeat(query, lax.ppermute(query, "x_lo", swap), NY)
    own = (key_stale, value_stale)
    up, down = [own], [own]
    for step in range(1, NZ // 2):
        up.append(tuple(move_z(array, 1) for array in up[-1]))
        down.append(tuple(move_z(array, -1) for array in down[-1]))
        if step == 1:
            up[1], down[1], stacked = lax.optimization_barrier((up[1], down[1], stacked))
            around = lax.all_to_all(stacked, "y", 0, 0)
    far = (move_z(up[-1][0], 1), move_z(down[-1][1], -1))
    partials = attend(
        ((2, 3), (4, 5), (6, 7), (1,), (0,)),
        jnp.stack([lax.axis_index("y"), lax.axis_index("x_lo")]).astype(jnp.int32),
        query,
        around,
        up + down[1:] + [far],
        key_fresh,
        value_fresh,
    )
    returned = lax.all_to_all(partials, ("y", "x_lo"), 0, 0)

    def block(x_half, core_half):
        return (x_half * 2 + core_half).astype(jnp.int32).reshape(1)

    attended, for_core, for_core_late = combine(
        jnp.concatenate([block(1 - x_hi, 1 - core), block(x_hi, 1 - core)]),
        returned,
        out_weight,
        columns,
    )
    from_core = lax.ppermute(for_core, "core", swap).astype(jnp.float32)
    chip_sum = project(block(1 - x_hi, core), attended, out_weight, columns, jnp.float32)
    chip_sum = (chip_sum + from_core).astype(jnp.bfloat16)
    from_x = lax.ppermute(chip_sum, "x_hi", swap)
    attended, for_core_late, _ = lax.optimization_barrier((attended, for_core_late, chip_sum))
    from_core = lax.ppermute(for_core_late, "core", swap)
    total = project(block(x_hi, core), attended, out_weight, columns, jnp.float32)
    total = total + from_core.astype(jnp.float32)
    total = total + from_x.astype(jnp.float32)
    return (
        residual.astype(jnp.float32) + gate.astype(jnp.float32)[None, :] * total
    ).astype(jnp.bfloat16)


def solution(mesh):
    axes = ("y", "x_lo", "z", "x_hi", "core")
    fine = Mesh(mesh.devices.reshape(NY, NX, NZ, 2, 2), axes)
    rows, cols = ("y", "x_lo", "z"), ("x_hi", "core")
    return jax.shard_map(
        shards,
        mesh=fine,
        in_specs=(
            P(rows, cols),
            P(rows, cols),
            P(rows, cols),
            P(rows, cols),
            P(rows, cols),
            P(cols, None),
            P(rows, cols),
            P(cols),
        ),
        out_specs=P(rows, cols),
        check_vma=False,
    )
```

time: 891 us -> 131 us (0.15)
  waiting for transfers between devices: 702 us -> 50.9 us
  local copies, waits for them, and re-layouts: 74.7 us -> 3.34 us
  matrix products: 64.8 us -> 0 us
  starting transfers between devices: 0.08 us -> 37.8 us
  Pallas kernels: 0 us -> 33.1 us
  other arithmetic: 31.1 us -> 4.81 us
  between operations: 13.2 us -> 0.11 us
    all_gather x2 -> x0, waiting for transfers between devices: 620 us -> none  [the longest x1 327 us: shards(): lax.all_gather(key_stale, 'patch', axis=0, tiled=True)]
    reduce_scatter x1 -> x0, waiting for transfers between devices: 80.8 us -> none  [shards(): lax.psum_scatter(partial_out.astype(jnp.bfloat16), 'head', scatter_dimens...]
    dynamic_slice x24 -> x0, local copies, waits for them, and re-layouts: 69.9 us -> none  [the longest x12 48 us: outer_step(): block_values = lax.dynamic_slice_in_dim(all_values, offset, block_size, 0)]
    dot_general x13 -> x0, matrix products: 64.8 us -> none  [the longest x6 32.9 us: absorb(): jnp.einsum('hqk,khd->hqd', weights.astype(jnp.bfloat16), value_cube, pref...]
    pallas_call x0 -> x5, Pallas kernels: none -> 33.1 us  [the longest x1 19.4 us: attend(): pl.pallas_call(functools.partial(attend_kernel, groups, 2 * count), in_sp...]
    ppermute x0 -> x18, starting transfers between devices: none -> 29.6 us  [the longest x14 19.4 us: move_z(): return lax.ppermute(array, 'z', [(z, (z + step) % NZ) for z in range(NZ)])]
    reduce_sum x6 -> x0, other arithmetic: 28.8 us -> none  [absorb(): running_sum = running_sum * rescale + jnp.sum(weights, axis=2)]
    ppermute x0 -> x18, waiting for transfers between devices: none -> 28.5 us  [the longest x14 20.2 us: move_z(): return lax.ppermute(array, 'z', [(z, (z + step) % NZ) for z in range(NZ)])]
  transfers between devices with their start and end apart: 3 -> 20, of which waited for: 3 -> 11; matrix products, arithmetic and copies ran while one was open for 0% -> 1% of each run, Pallas kernels for 0% -> 7%
where the time goes in v2:
time: 131 us; the launch traced here: 130 us
  waiting for transfers between devices  50.9 us (39%)
  starting transfers between devices  37.8 us (29%)
  Pallas kernels  33.1 us (25%)
  other arithmetic  4.81 us (4%)
  local copies, waits for them, and re-layouts  3.34 us (3%)
    all_to_all x1, waiting for transfers between devices, shards(): returned = lax.all_to_all(partials, ('y', 'x_lo'), 0, 0)  22.4 us
    ppermute x14, waiting for transfers between devices, move_z(): return lax.ppermute(array, 'z', [(z, (z + step) % NZ) for z in range(NZ)])  20.2 us
    ppermute x14, starting transfers between devices, move_z(): return lax.ppermute(array, 'z', [(z, (z + step) % NZ) for z in range(NZ)])  19.4 us
    pallas_call x1, Pallas kernels, attend(): pl.pallas_call(functools.partial(attend_kernel, groups, 2 * count), in_sp...  19.4 us
    ppermute x1, waiting for transfers between devices, shards(): from_x = lax.ppermute(chip_sum, 'x_hi', swap)  8.29 us
    pallas_call x2, Pallas kernels, project(): pl.pallas_call(project_kernel, grid_spec=pltpu.PrefetchScalarGridSpec(num...  5.76 us
    ppermute x1, starting transfers between devices, shards(): from_core = lax.ppermute(for_core, 'core', swap).astype(jnp.float32)  5.28 us
    pallas_call x1, Pallas kernels, combine(): pl.pallas_call(combine_kernel, in_specs=[pl.BlockSpec(memory_space=pltpu....  5.11 us
  transfers between devices with their start and end apart: 20, of which 11 were waited for; matrix products, arithmetic and copies ran while one was open for 1% of the time, Pallas kernels for 7%

profile of v2, /device:TPU:1, one launch (start us, length us, event | category | flops | bytes accessed | tf_op | source)
XLA Modules:
  0.0 130.1 jit_solution(14978057914570596238)
XLA Ops:
  0.0 2.0 %collective-permute-start.4 = (bf16[192,640]{1,0:T(8,128)(2,1)}, bf16[192,640]{1,0:T(8,128)(2,1)S(1)}, u32[]{:S(2)}, u32[]{:S(2)}) collective-permute-start(bf16[192,640]{1,0:T(8,128)(2,1)} %query_ref.1), channel_id=1, source_target_pairs={{0,32},{32,0},{1,33},{33,1},{2,34},{34,2},{3,35},{35,3},{4,36},{36... | collective-permute-start | bytes 737288 | tf_op jit(solution)/shard_map/ppermute | solution.py:310
  3.7 1.6 %collective-permute-start.1 = (bf16[192,640]{1,0:T(8,128)(2,1)}, bf16[192,640]{1,0:T(8,128)(2,1)S(1)}, u32[]{:S(2)}, u32[]{:S(2)}) collective-permute-start(bf16[192,640]{1,0:T(8,128)(2,1)} %refs_1_.1), channel_id=1, source_target_pairs={{0,4},{4,8},{8,12},{12,16},{16,20},{20,24},{24,28},{28,0},{1,5},{5... | collective-permute-start | bytes 737288 | tf_op jit(solution)/shard_map/ppermute | solution.py:302
  5.3 2.3 %collective-permute-start.2 = (bf16[192,640]{1,0:T(8,128)(2,1)}, bf16[192,640]{1,0:T(8,128)(2,1)S(1)}, u32[]{:S(2)}, u32[]{:S(2)}) collective-permute-start(bf16[192,640]{1,0:T(8,128)(2,1)} %refs_0_.1), channel_id=1, source_target_pairs={{0,28},{4,0},{8,4},{12,8},{16,12},{20,16},{24,20},{28,24},{1,29},{... | collective-permute-start | bytes 737288 | tf_op jit(solution)/shard_map/ppermute | solution.py:302
  9.8 2.9 %repeat.1 = bf16[4,384,640]{2,1,0:T(8,128)(2,1)} custom-call(bf16[192,640]{1,0:T(8,128)(2,1)} %query_ref.1, bf16[192,640]{1,0:T(8,128)(2,1)} %copy-done.3), custom_call_target="tpu_custom_call" | custom-call | tf_op jit(solution)/shard_map/repeat/pallas_call | solution.py:197
  13.2 5.3 %collective-permute-done.1.refs_3_ = bf16[192,640]{1,0:T(8,128)(2,1)S(1)} collective-permute-done((bf16[192,640]{1,0:T(8,128)(2,1)}, bf16[192,640]{1,0:T(8,128)(2,1)S(1)}, u32[]{:S(2)}, u32[]{:S(2)}) %collective-permute-start.1) | collective-permute-done | bytes 245792 | tf_op jit(solution)/shard_map/ppermute | solution.py:302
  18.5 4.2 %all-to-all-start = ((bf16[4,384,640]{2,1,0:T(8,128)(2,1)}), bf16[4,384,640]{2,1,0:T(8,128)(2,1)S(1)}, u32[]{:S(2)}, u32[]{:S(2)}) async-start(bf16[4,384,640]{2,1,0:T(8,128)(2,1)} %repeat.1), calls=%async_computation | async-start | bytes 3932160 | tf_op jit(solution)/shard_map/all_to_all | solution.py:318
  26.8 2.7 %collective-permute-done.5.refs_4_ = bf16[192,640]{1,0:T(8,128)(2,1)S(1)} collective-permute-done((bf16[192,640]{1,0:T(8,128)(2,1)S(1)}, bf16[192,640]{1,0:T(8,128)(2,1)S(1)}, u32[]{:S(2)}, u32[]{:S(2)}) %collective-permute-start.5) | collective-permute-done | bytes 245792 | tf_op jit(solution)/shard_map/ppermute | solution.py:302
  29.6 2.6 %collective-permute-start.12 = (bf16[192,640]{1,0:T(8,128)(2,1)S(1)}, bf16[192,640]{1,0:T(8,128)(2,1)}, u32[]{:S(2)}, u32[]{:S(2)}) collective-permute-start(bf16[192,640]{1,0:T(8,128)(2,1)S(1)} %collective-permute-done.10.refs_11_), channel_id=1, source_target_pairs={{0,28},{4,0},{8,4},{12,8},{16,12},{20,16},{24,20},{28,24},{1,29},{... | collective-permute-start | bytes 737288 | tf_op jit(solution)/shard_map/ppermute | solution.py:302
  32.2 2.1 %collective-permute-done.9.refs_10_ = bf16[192,640]{1,0:T(8,128)(2,1)} collective-permute-done((bf16[192,640]{1,0:T(8,128)(2,1)S(1)}, bf16[192,640]{1,0:T(8,128)(2,1)}, u32[]{:S(2)}, u32[]{:S(2)}) %collective-permute-start.9) | collective-permute-done | bytes 245792 | tf_op jit(solution)/shard_map/ppermute | solution.py:302
  34.3 2.9 %collective-permute-start.11 = (bf16[192,640]{1,0:T(8,128)(2,1)}, bf16[192,640]{1,0:T(8,128)(2,1)}, u32[]{:S(2)}, u32[]{:S(2)}) collective-permute-start(bf16[192,640]{1,0:T(8,128)(2,1)} %collective-permute-done.9.refs_10_), channel_id=1, source_target_pairs={{0,28},{4,0},{8,4},{12,8},{16,12},{20,16},{24,20},{28,24},{1,29},{... | collective-permute-start | bytes 737288 | tf_op jit(solution)/shard_map/ppermute | solution.py:302
  37.2 3.3 %collective-permute-done.7.refs_6_ = bf16[192,640]{1,0:T(8,128)(2,1)} collective-permute-done((bf16[192,640]{1,0:T(8,128)(2,1)S(1)}, bf16[192,640]{1,0:T(8,128)(2,1)}, u32[]{:S(2)}, u32[]{:S(2)}) %collective-permute-start.7) | collective-permute-done | bytes 245792 | tf_op jit(solution)/shard_map/ppermute | solution.py:302
  40.5 2.7 %collective-permute-start.14 = (bf16[192,640]{1,0:T(8,128)(2,1)}, bf16[192,640]{1,0:T(8,128)(2,1)}, u32[]{:S(2)}, u32[]{:S(2)}) collective-permute-start(bf16[192,640]{1,0:T(8,128)(2,1)} %collective-permute-done.12.refs_13_), channel_id=1, source_target_pairs={{0,28},{4,0},{8,4},{12,8},{16,12},{20,16},{24,20},{28,24},{1,29},{... | collective-permute-start | bytes 737288 | tf_op jit(solution)/shard_map/ppermute | solution.py:302
  45.0 2.6 %collective-permute-done.13.refs_14_ = bf16[192,640]{1,0:T(8,128)(2,1)} collective-permute-done((bf16[192,640]{1,0:T(8,128)(2,1)}, bf16[192,640]{1,0:T(8,128)(2,1)}, u32[]{:S(2)}, u32[]{:S(2)}) %collective-permute-start.13) | collective-permute-done | bytes 245792 | tf_op jit(solution)/shard_map/ppermute | solution.py:302
  47.7 2.5 %collective-permute-done.14.refs_15_ = bf16[192,640]{1,0:T(8,128)(2,1)} collective-permute-done((bf16[192,640]{1,0:T(8,128)(2,1)}, bf16[192,640]{1,0:T(8,128)(2,1)}, u32[]{:S(2)}, u32[]{:S(2)}) %collective-permute-start.14) | collective-permute-done | bytes 245792 | tf_op jit(solution)/shard_map/ppermute | solution.py:302
  51.4 19.4 %attend.1 = bf16[8,208,640]{2,1,0:T(8,128)(2,1)} custom-call(s32[2]{0:T(128)} %pad_add_fusion.1.place_ref, bf16[192,640]{1,0:T(8,128)(2,1)} %query_ref.1, bf16[4,384,640]{2,1,0:T(8,128)(2,1)} %copy-done.1, bf16[192,640]{1,0:T(8,128)(2,1)} %refs_0_.1, bf16[192,640]{1,0:T(8,128)(2,1)} %refs_1_.1, bf16[192,640]{1,0:T(8,128)(2,1)} %copy-done.6, ...), custom_call_target="tpu_custom_call" | custom-call | flops 24159191040 | tf_op jit(solution)/shard_map/attend/pallas_call | solution.py:161
  70.8 4.0 %all-to-all-start.1 = ((bf16[8,208,640]{2,1,0:T(8,128)(2,1)}), bf16[8,208,640]{2,1,0:T(8,128)(2,1)S(1)}, u32[]{:S(2)}, u32[]{:S(2)}) async-start(bf16[8,208,640]{2,1,0:T(8,128)(2,1)} %attend.1), calls=%async_computation.1 | async-start | bytes 4259840 | tf_op jit(solution)/shard_map/all_to_all | solution.py:329
  75.5 22.4 %all-to-all-done.1.parts_ref = bf16[8,208,640]{2,1,0:T(8,128)(2,1)S(1)} async-done(((bf16[8,208,640]{2,1,0:T(8,128)(2,1)}), bf16[8,208,640]{2,1,0:T(8,128)(2,1)S(1)}, u32[]{:S(2)}, u32[]{:S(2)}) %all-to-all-start.1) | async-done | bytes 2129952 | tf_op jit(solution)/shard_map/all_to_all | solution.py:329
  99.2 5.1 %combine.1 = (bf16[192,640]{1,0:T(8,128)(2,1)}, bf16[192,1280]{1,0:T(8,128)(2,1)}, bf16[192,1280]{1,0:T(8,128)(2,1)}) custom-call(s32[2]{0:T(128)} %pad_add_fusion.blocks_ref, bf16[8,208,640]{2,1,0:T(8,128)(2,1)} %copy-done, bf16[640,5120]{1,0:T(8,128)(2,1)} %w_ref.5), custom_call_target="tpu_custom_call" | custom-call | tf_op jit(solution)/shard_map/combine/pallas_call | solution.py:252
  104.3 5.3 %collective-permute-start.15 = (bf16[192,1280]{1,0:T(8,128)(2,1)}, bf16[192,1280]{1,0:T(8,128)(2,1)S(1)}, u32[]{:S(2)}, u32[]{:S(2)}) collective-permute-start(bf16[192,1280]{1,0:T(8,128)(2,1)} %get-tuple-element.22), channel_id=1, source_target_pairs={{0,1},{1,0},{2,3},{3,2},{4,5},{5,4},{6,7},{7,6},{8,9},{9,8},{10,11... | collective-permute-start | bytes 1474568 | tf_op jit(solution)/shard_map/ppermute | solution.py:340
  109.6 2.9 %project.2 = f32[192,1280]{1,0:T(8,128)} custom-call(s32[1]{0:T(128)} %bitcast.5.block_ref, bf16[192,640]{1,0:T(8,128)(2,1)} %get-tuple-element.23.a_ref, bf16[640,5120]{1,0:T(8,128)(2,1)} %w_ref.5), custom_call_target="tpu_custom_call" | custom-call | tf_op jit(solution)/shard_map/project/pallas_call | solution.py:284
  113.9 2.8 %collective-permute-start.17 = (bf16[192,1280]{1,0:T(8,128)(2,1)S(1)}, bf16[192,1280]{1,0:T(8,128)(2,1)S(1)}, u32[]{:S(2)}, u32[]{:S(2)}) collective-permute-start(bf16[192,1280]{1,0:T(8,128)(2,1)S(1)} %add_convert_fusion.1), channel_id=1, source_target_pairs={{0,2},{2,0},{1,3},{3,1},{4,6},{6,4},{5,7},{7,5},{8,10},{10,8},{9,1... | collective-permute-start | bytes 1474568 | tf_op jit(solution)/shard_map/ppermute | solution.py:343
  116.7 2.9 %project.3 = f32[192,1280]{1,0:T(8,128)} custom-call(s32[1]{0:T(128)} %bitcast.block_ref, bf16[192,640]{1,0:T(8,128)(2,1)} %get-tuple-element.23.a_ref, bf16[640,5120]{1,0:T(8,128)(2,1)} %w_ref.5), custom_call_target="tpu_custom_call" | custom-call | tf_op jit(solution)/shard_map/project/pallas_call | solution.py:284
  119.6 8.3 %collective-permute-done.17 = bf16[192,1280]{1,0:T(8,128)(2,1)S(1)} collective-permute-done((bf16[192,1280]{1,0:T(8,128)(2,1)S(1)}, bf16[192,1280]{1,0:T(8,128)(2,1)S(1)}, u32[]{:S(2)}, u32[]{:S(2)}) %collective-permute-start.17) | collective-permute-done | bytes 491552 | tf_op jit(solution)/shard_map/ppermute | solution.py:343
  127.9 2.2 %add_convert_fusion = bf16[192,1280]{1,0:T(8,128)(2,1)} fusion(bf16[192,1280]{1,0:T(8,128)(2,1)S(1)} %collective-permute-done.17, f32[192,1280]{1,0:T(8,128)} %project.3, bf16[192,1280]{1,0:T(8,128)(2,1)S(1)} %collective-permute-done.16, bf16[192,1280]{1,0:T(8,128)(2,1)S(1)} %copy-done.2, f32[1280]{0:T(1024)S(1)} %convert_element_type.22), kind=kLoop, calls=%fused_computation | loop fusion | flops 1966080 | bytes 2954240 | tf_op jit(solution)/shard_map/convert_element_type | solution.py:351
  (50 shorter events, 15.1 us)
Async XLA Ops:
  0.0 9.1 %collective-permute-start.4 = (bf16[192,640]{1,0:T(8,128)(2,1)}, bf16[192,640]{1,0:T(8,128)(2,1)S(1)}, u32[]{:S(2)}, u32[]{:S(2)}) collective-permute-start(bf16[192,640]{1,0:T(8,128)(2,1)} %query_ref.1), channel_id=1, source_target_pairs={{0,32},{32,0},{1,33},{33,1},{2,34},{34,2},{3,35},{35,3},{4,36},{36... | collective-permute-start | bytes 737288 | tf_op jit(solution)/shard_map/ppermute | solution.py:310
  2.0 11.1 %collective-permute-start = (bf16[192,640]{1,0:T(8,128)(2,1)}, bf16[192,640]{1,0:T(8,128)(2,1)S(1)}, u32[]{:S(2)}, u32[]{:S(2)}) collective-permute-start(bf16[192,640]{1,0:T(8,128)(2,1)} %refs_0_.1), channel_id=1, source_target_pairs={{0,4},{4,8},{8,12},{12,16},{16,20},{20,24},{24,28},{28,0},{1,5},{5... | collective-permute-start | bytes 737288 | tf_op jit(solution)/shard_map/ppermute | solution.py:302
  3.7 14.8 %collective-permute-start.1 = (bf16[192,640]{1,0:T(8,128)(2,1)}, bf16[192,640]{1,0:T(8,128)(2,1)S(1)}, u32[]{:S(2)}, u32[]{:S(2)}) collective-permute-start(bf16[192,640]{1,0:T(8,128)(2,1)} %refs_1_.1), channel_id=1, source_target_pairs={{0,4},{4,8},{8,12},{12,16},{16,20},{20,24},{24,28},{28,0},{1,5},{5... | collective-permute-start | bytes 737288 | tf_op jit(solution)/shard_map/ppermute | solution.py:302
  5.3 13.1 %collective-permute-start.2 = (bf16[192,640]{1,0:T(8,128)(2,1)}, bf16[192,640]{1,0:T(8,128)(2,1)S(1)}, u32[]{:S(2)}, u32[]{:S(2)}) collective-permute-start(bf16[192,640]{1,0:T(8,128)(2,1)} %refs_0_.1), channel_id=1, source_target_pairs={{0,28},{4,0},{8,4},{12,8},{16,12},{20,16},{24,20},{28,24},{1,29},{... | collective-permute-start | bytes 737288 | tf_op jit(solution)/shard_map/ppermute | solution.py:302
  7.6 10.8 %collective-permute-start.3 = (bf16[192,640]{1,0:T(8,128)(2,1)}, bf16[192,640]{1,0:T(8,128)(2,1)S(1)}, u32[]{:S(2)}, u32[]{:S(2)}) collective-permute-start(bf16[192,640]{1,0:T(8,128)(2,1)} %refs_1_.1), channel_id=1, source_target_pairs={{0,28},{4,0},{8,4},{12,8},{16,12},{20,16},{24,20},{28,24},{1,29},{... | collective-permute-start | bytes 737288 | tf_op jit(solution)/shard_map/ppermute | solution.py:302
  13.2 36.9 %copy-start.6 = (bf16[192,640]{1,0:T(8,128)(2,1)}, bf16[192,640]{1,0:T(8,128)(2,1)S(1)}, u32[]{:S(2)}) copy-start(bf16[192,640]{1,0:T(8,128)(2,1)S(1)} %collective-permute-done.refs_2_) | copy-start | bytes 737284
  18.5 31.7 %copy-start.7 = (bf16[192,640]{1,0:T(8,128)(2,1)}, bf16[192,640]{1,0:T(8,128)(2,1)S(1)}, u32[]{:S(2)}) copy-start(bf16[192,640]{1,0:T(8,128)(2,1)S(1)} %collective-permute-done.1.refs_3_) | copy-start | bytes 737284
  18.5 31.7 %copy-start.8 = (bf16[192,640]{1,0:T(8,128)(2,1)}, bf16[192,640]{1,0:T(8,128)(2,1)S(1)}, u32[]{:S(2)}) copy-start(bf16[192,640]{1,0:T(8,128)(2,1)S(1)} %collective-permute-done.2.refs_8_) | copy-start | bytes 737284
  18.5 31.7 %copy-start.9 = (bf16[192,640]{1,0:T(8,128)(2,1)}, bf16[192,640]{1,0:T(8,128)(2,1)S(1)}, u32[]{:S(2)}) copy-start(bf16[192,640]{1,0:T(8,128)(2,1)S(1)} %collective-permute-done.3.refs_9_) | copy-start | bytes 737284
  18.5 31.6 %all-to-all-start = ((bf16[4,384,640]{2,1,0:T(8,128)(2,1)}), bf16[4,384,640]{2,1,0:T(8,128)(2,1)S(1)}, u32[]{:S(2)}, u32[]{:S(2)}) async-start(bf16[4,384,640]{2,1,0:T(8,128)(2,1)} %repeat.1), calls=%async_computation | async-start | bytes 3932160 | tf_op jit(solution)/shard_map/all_to_all | solution.py:318
  22.7 6.8 %collective-permute-start.5 = (bf16[192,640]{1,0:T(8,128)(2,1)S(1)}, bf16[192,640]{1,0:T(8,128)(2,1)S(1)}, u32[]{:S(2)}, u32[]{:S(2)}) collective-permute-start(bf16[192,640]{1,0:T(8,128)(2,1)S(1)} %collective-permute-done.refs_2_), channel_id=1, source_target_pairs={{0,4},{4,8},{8,12},{12,16},{16,20},{20,24},{24,28},{28,0},{1,5},{5... | collective-permute-start | bytes 737288 | tf_op jit(solution)/shard_map/ppermute | solution.py:302
  24.2 5.3 %collective-permute-start.10 = (bf16[192,640]{1,0:T(8,128)(2,1)S(1)}, bf16[192,640]{1,0:T(8,128)(2,1)S(1)}, u32[]{:S(2)}, u32[]{:S(2)}) collective-permute-start(bf16[192,640]{1,0:T(8,128)(2,1)S(1)} %collective-permute-done.3.refs_9_), channel_id=1, source_target_pairs={{0,28},{4,0},{8,4},{12,8},{16,12},{20,16},{24,20},{28,24},{1,29},{... | collective-permute-start | bytes 737288 | tf_op jit(solution)/shard_map/ppermute | solution.py:302
  25.4 9.0 %collective-permute-start.9 = (bf16[192,640]{1,0:T(8,128)(2,1)S(1)}, bf16[192,640]{1,0:T(8,128)(2,1)}, u32[]{:S(2)}, u32[]{:S(2)}) collective-permute-start(bf16[192,640]{1,0:T(8,128)(2,1)S(1)} %collective-permute-done.2.refs_8_), channel_id=1, source_target_pairs={{0,28},{4,0},{8,4},{12,8},{16,12},{20,16},{24,20},{28,24},{1,29},{... | collective-permute-start | bytes 737288 | tf_op jit(solution)/shard_map/ppermute | solution.py:302
  26.5 10.7 %collective-permute-start.6 = (bf16[192,640]{1,0:T(8,128)(2,1)S(1)}, bf16[192,640]{1,0:T(8,128)(2,1)}, u32[]{:S(2)}, u32[]{:S(2)}) collective-permute-start(bf16[192,640]{1,0:T(8,128)(2,1)S(1)} %collective-permute-done.1.refs_3_), channel_id=1, source_target_pairs={{0,4},{4,8},{8,12},{12,16},{16,20},{20,24},{24,28},{28,0},{1,5},{5... | collective-permute-start | bytes 737288 | tf_op jit(solution)/shard_map/ppermute | solution.py:302
  29.5 10.9 %collective-permute-start.7 = (bf16[192,640]{1,0:T(8,128)(2,1)S(1)}, bf16[192,640]{1,0:T(8,128)(2,1)}, u32[]{:S(2)}, u32[]{:S(2)}) collective-permute-start(bf16[192,640]{1,0:T(8,128)(2,1)S(1)} %collective-permute-done.5.refs_4_), channel_id=1, source_target_pairs={{0,4},{4,8},{8,12},{12,16},{16,20},{20,24},{24,28},{28,0},{1,5},{5... | collective-permute-start | bytes 737288 | tf_op jit(solution)/shard_map/ppermute | solution.py:302
  29.6 10.9 %collective-permute-start.12 = (bf16[192,640]{1,0:T(8,128)(2,1)S(1)}, bf16[192,640]{1,0:T(8,128)(2,1)}, u32[]{:S(2)}, u32[]{:S(2)}) collective-permute-start(bf16[192,640]{1,0:T(8,128)(2,1)S(1)} %collective-permute-done.10.refs_11_), channel_id=1, source_target_pairs={{0,28},{4,0},{8,4},{12,8},{16,12},{20,16},{24,20},{28,24},{1,29},{... | collective-permute-start | bytes 737288 | tf_op jit(solution)/shard_map/ppermute | solution.py:302
  34.3 10.5 %collective-permute-start.11 = (bf16[192,640]{1,0:T(8,128)(2,1)}, bf16[192,640]{1,0:T(8,128)(2,1)}, u32[]{:S(2)}, u32[]{:S(2)}) collective-permute-start(bf16[192,640]{1,0:T(8,128)(2,1)} %collective-permute-done.9.refs_10_), channel_id=1, source_target_pairs={{0,28},{4,0},{8,4},{12,8},{16,12},{20,16},{24,20},{28,24},{1,29},{... | collective-permute-start | bytes 737288 | tf_op jit(solution)/shard_map/ppermute | solution.py:302
  37.2 7.9 %collective-permute-start.8 = (bf16[192,640]{1,0:T(8,128)(2,1)}, bf16[192,640]{1,0:T(8,128)(2,1)}, u32[]{:S(2)}, u32[]{:S(2)}) collective-permute-start(bf16[192,640]{1,0:T(8,128)(2,1)} %collective-permute-done.6.refs_5_), channel_id=1, source_target_pairs={{0,4},{4,8},{8,12},{12,16},{16,20},{20,24},{24,28},{28,0},{1,5},{5... | collective-permute-start | bytes 737288 | tf_op jit(solution)/shard_map/ppermute | solution.py:302
  40.5 7.2 %collective-permute-start.13 = (bf16[192,640]{1,0:T(8,128)(2,1)}, bf16[192,640]{1,0:T(8,128)(2,1)}, u32[]{:S(2)}, u32[]{:S(2)}) collective-permute-start(bf16[192,640]{1,0:T(8,128)(2,1)} %collective-permute-done.7.refs_6_), channel_id=1, source_target_pairs={{0,4},{4,8},{8,12},{12,16},{16,20},{20,24},{24,28},{28,0},{1,5},{5... | collective-permute-start | bytes 737288 | tf_op jit(solution)/shard_map/ppermute | solution.py:302
  40.5 9.7 %collective-permute-start.14 = (bf16[192,640]{1,0:T(8,128)(2,1)}, bf16[192,640]{1,0:T(8,128)(2,1)}, u32[]{:S(2)}, u32[]{:S(2)}) collective-permute-start(bf16[192,640]{1,0:T(8,128)(2,1)} %collective-permute-done.12.refs_13_), channel_id=1, source_target_pairs={{0,28},{4,0},{8,4},{12,8},{16,12},{20,16},{24,20},{28,24},{1,29},{... | collective-permute-start | bytes 737288 | tf_op jit(solution)/shard_map/ppermute | solution.py:302
  70.8 27.1 %all-to-all-start.1 = ((bf16[8,208,640]{2,1,0:T(8,128)(2,1)}), bf16[8,208,640]{2,1,0:T(8,128)(2,1)S(1)}, u32[]{:S(2)}, u32[]{:S(2)}) async-start(bf16[8,208,640]{2,1,0:T(8,128)(2,1)} %attend.1), calls=%async_computation.1 | async-start | bytes 4259840 | tf_op jit(solution)/shard_map/all_to_all | solution.py:329
  104.3 8.2 %collective-permute-start.15 = (bf16[192,1280]{1,0:T(8,128)(2,1)}, bf16[192,1280]{1,0:T(8,128)(2,1)S(1)}, u32[]{:S(2)}, u32[]{:S(2)}) collective-permute-start(bf16[192,1280]{1,0:T(8,128)(2,1)} %get-tuple-element.22), channel_id=1, source_target_pairs={{0,1},{1,0},{2,3},{3,2},{4,5},{5,4},{6,7},{7,6},{8,9},{9,8},{10,11... | collective-permute-start | bytes 1474568 | tf_op jit(solution)/shard_map/ppermute | solution.py:340
  113.8 5.8 %collective-permute-start.16 = (bf16[192,1280]{1,0:T(8,128)(2,1)S(1)}, bf16[192,1280]{1,0:T(8,128)(2,1)S(1)}, u32[]{:S(2)}, u32[]{:S(2)}) collective-permute-start(bf16[192,1280]{1,0:T(8,128)(2,1)S(1)} %copy-done.5), channel_id=1, source_target_pairs={{0,1},{1,0},{2,3},{3,2},{4,5},{5,4},{6,7},{7,6},{8,9},{9,8},{10,11... | collective-permute-start | bytes 1474568 | tf_op jit(solution)/shard_map/ppermute | solution.py:345
  113.9 14.0 %collective-permute-start.17 = (bf16[192,1280]{1,0:T(8,128)(2,1)S(1)}, bf16[192,1280]{1,0:T(8,128)(2,1)S(1)}, u32[]{:S(2)}, u32[]{:S(2)}) collective-permute-start(bf16[192,1280]{1,0:T(8,128)(2,1)S(1)} %add_convert_fusion.1), channel_id=1, source_target_pairs={{0,2},{2,0},{1,3},{3,1},{4,6},{6,4},{5,7},{7,5},{8,10},{10,8},{9,1... | collective-permute-start | bytes 1474568 | tf_op jit(solution)/shard_map/ppermute | solution.py:343
  (8 other events, 67.0 us)

commit v3 on v2

--- a/solution.py
+++ b/solution.py
@@ -85,13 +85,14 @@
     return jnp.concatenate(stat, axis=0).astype(jnp.bfloat16)
 
 
-def attend_kernel(groups, blocks, place_ref, query_ref, around_ref, *refs):
+def attend_kernel(groups, blocks, first_head, place_ref, query_ref, around_ref, *refs):
     block_refs, refs = refs[:blocks], refs[blocks:]
     k_refs, v_refs = block_refs[::2], block_refs[1::2]
     fresh_k_ref, fresh_v_ref, out_ref, refs = *refs[:3], refs[3:]
     q_buf, k_buf, v_buf, fresh_k, fresh_v, out_buf, sems = refs
-    rows, width = query_ref.shape
+    rows, width = fresh_k.shape
     heads = width // HD
+    taken = pl.ds(first_head * HD, width)
     arrivals = Arrivals(sems)
     got_q = {}
     y, x = place_ref[0], place_ref[1]
@@ -107,18 +108,18 @@
         first, count = group[0], len(group)
         if first:
             dx = OFFSETS[first][1]
-            from_ref = around_ref.at[source(first)[0], pl.ds(dx * rows, count * rows)]
+            from_ref = around_ref.at[source(first)[0], pl.ds(dx * rows, count * rows), taken]
         else:
-            from_ref = query_ref
+            from_ref = query_ref.at[:, taken]
         got_q[group] = arrivals.start(from_ref, q_buf.at[lines(first, count)])
 
     fetch(groups[0])
-    got_k = [arrivals.start(ref, k_buf.at[lines(i)]) for i, ref in enumerate(k_refs)]
-    got_v = [arrivals.start(ref, v_buf.at[lines(i)]) for i, ref in enumerate(v_refs)]
+    got_k = [arrivals.start(ref.at[:, taken], k_buf.at[lines(i)]) for i, ref in enumerate(k_refs)]
+    got_v = [arrivals.start(ref.at[:, taken], v_buf.at[lines(i)]) for i, ref in enumerate(v_refs)]
     for group in groups[1:]:
         fetch(group)
-    got_fresh_k = arrivals.start(fresh_k_ref, fresh_k)
-    got_fresh_v = arrivals.start(fresh_v_ref, fresh_v)
+    got_fresh_k = arrivals.start(fresh_k_ref.at[:, taken], fresh_k)
+    got_fresh_v = arrivals.start(fresh_v_ref.at[:, taken], fresh_v)
     tiles = [(group, head) for group in groups for head in range(heads)]
 
     def scores_of(i):
@@ -154,12 +155,12 @@
     arrivals.wait(*range(len(arrivals.copies)))
 
 
-def attend(groups, place, query, around, blocks, fresh_key, fresh_value):
-    rows, width = query.shape
+def attend(groups, heads, place, query, around, blocks, fresh_key, fresh_value):
+    rows, width = query.shape[0], len(heads) * HD
     slots, count = len(OFFSETS), len(blocks)
     anywhere = pl.BlockSpec(memory_space=pl.ANY)
     return pl.pallas_call(
-        functools.partial(attend_kernel, groups, 2 * count),
+        functools.partial(attend_kernel, groups, 2 * count, heads[0]),
         in_specs=[pl.BlockSpec(memory_space=pltpu.SMEM)] + [anywhere] * (4 + 2 * count),
         out_specs=anywhere,
         out_shape=jax.ShapeDtypeStruct((slots, rows + STAT_ROWS, width), jnp.bfloat16),
@@ -185,6 +186,23 @@
     )
 
 
+def last_kernel(place_ref, keys_ref, values_ref, out_ref):
+    for i in range(out_ref.shape[0]):
+        out_ref[i] = place_ref[i]
+
+
+def last_of(place, keys, values):
+    smem, anywhere = pl.BlockSpec(memory_space=pltpu.SMEM), pl.BlockSpec(memory_space=pl.ANY)
+    return pl.pallas_call(
+        last_kernel,
+        in_specs=[smem, anywhere, anywhere],
+        out_specs=smem,
+        out_shape=jax.ShapeDtypeStruct(place.shape, place.dtype),
+        cost_estimate=pl.CostEstimate(flops=13 * 10**9, bytes_accessed=0, transcendentals=0),
+        name="last_of",
+    )(place, keys, values)
+
+
 def repeat_kernel(a_ref, b_ref, out_ref):
     rows = a_ref.shape[0]
     out_ref[:rows, :] = a_ref[...]
@@ -205,7 +223,8 @@
     )(a, b)
 
 
-def combine_kernel(blocks_ref, parts_ref, w_ref, out_ref, first_ref, second_ref, w_buf, sems):
+def combine_kernel(blocks_ref, w_ref, *refs):
+    *parts_refs, out_ref, first_ref, second_ref, w_buf, sems = refs
     product_refs = (first_ref, second_ref)
     columns = first_ref.shape[1]
     copies = []
@@ -214,12 +233,12 @@
         copy = pltpu.make_async_copy(w_ref.at[:, pl.ds(first, columns)], w_buf.at[i], sems.at[i])
         copy.start()
         copies.append(copy)
-    group = parts_ref.shape[0]
+    group = parts_refs[0].shape[0]
     rows, width = out_ref.shape
     heads = width // HD
+    where = [(ref, head_columns(i)) for ref in parts_refs for i in range(ref.shape[2] // HD)]
     shares = []
-    for head in range(heads):
-        columns = slice(head * HD, (head + 1) * HD)
+    for parts_ref, columns in where:
         lse = []
         for part in range(group):
             stat = parts_ref[part, rows:, columns].astype(jnp.float32)
@@ -230,14 +249,13 @@
         shares.append(share / jnp.sum(share, axis=0, keepdims=True))
     shares.append(jnp.zeros((HD - heads * group, rows), jnp.float32))
     by_row = jnp.transpose(jnp.concatenate(shares, axis=0))
-    for head in range(heads):
-        columns = slice(head * HD, (head + 1) * HD)
+    for head, (parts_ref, columns) in enumerate(where):
         total = jnp.zeros((rows, HD), jnp.float32)
         for part in range(group):
             at = head * group + part
             mixture = parts_ref[part, :rows, columns].astype(jnp.float32)
             total = total + by_row[:, at : at + 1] * mixture
-        out_ref[:, columns] = total.astype(jnp.bfloat16)
+        out_ref[:, head_columns(head)] = total.astype(jnp.bfloat16)
     for i, product_ref in enumerate(product_refs):
         copies[i].wait()
         product_ref[...] = jnp.dot(
@@ -246,15 +264,15 @@
 
 
 def combine(blocks, parts, out_weight, columns):
-    _, rows, width = parts.shape
-    rows -= STAT_ROWS
+    rows = parts[0].shape[1] - STAT_ROWS
+    width = sum(part.shape[2] for part in parts)
     vmem = pl.BlockSpec(memory_space=pltpu.VMEM)
     return pl.pallas_call(
         combine_kernel,
         in_specs=[
             pl.BlockSpec(memory_space=pltpu.SMEM),
-            vmem,
             pl.BlockSpec(memory_space=pl.ANY),
+            *[vmem] * len(parts),
         ],
         out_specs=[vmem, vmem, vmem],
         out_shape=[
@@ -268,7 +286,7 @@
         ],
         compiler_params=pltpu.CompilerParams(vmem_limit_bytes=BIG * 2**20),
         name="combine",
-    )(blocks, parts, out_weight)
+    )(blocks, out_weight, *parts)
 
 
 def project_kernel(block_ref, a_ref, w_ref, out_ref):
@@ -313,20 +331,23 @@
     for step in range(1, NZ // 2):
         up.append(tuple(move_z(array, 1) for array in up[-1]))
         down.append(tuple(move_z(array, -1) for array in down[-1]))
-        if step == 1:
-            up[1], down[1], stacked = lax.optimization_barrier((up[1], down[1], stacked))
-            around = lax.all_to_all(stacked, "y", 0, 0)
+    stacked = lax.optimization_barrier((stacked, up[1][0], down[1][0]))[0]
+    around = lax.all_to_all(stacked, "y", 0, 0)
     far = (move_z(up[-1][0], 1), move_z(down[-1][1], -1))
+    place = jnp.stack([lax.axis_index("y"), lax.axis_index("x_lo")]).astype(jnp.int32)
+    place = last_of(place, *far)
+    heads = query.shape[1] // HD
     partials = attend(
         ((2, 3), (4, 5), (6, 7), (1,), (0,)),
-        jnp.stack([lax.axis_index("y"), lax.axis_index("x_lo")]).astype(jnp.int32),
+        range(heads),
+        place,
         query,
         around,
         up + down[1:] + [far],
         key_fresh,
         value_fresh,
     )
-    returned = lax.all_to_all(partials, ("y", "x_lo"), 0, 0)
+    returned = [lax.all_to_all(partials, ("y", "x_lo"), 0, 0)]
 
     def block(x_half, core_half):
         return (x_half * 2 + core_half).astype(jnp.int32).reshape(1)
@@ -344,11 +365,10 @@
     attended, for_core_late, _ = lax.optimization_barrier((attended, for_core_late, chip_sum))
     from_core = lax.ppermute(for_core_late, "core", swap)
     total = project(block(x_hi, core), attended, out_weight, columns, jnp.float32)
+    gate_row = gate.astype(jnp.float32)[None, :]
     total = total + from_core.astype(jnp.float32)
-    total = total + from_x.astype(jnp.float32)
-    return (
-        residual.astype(jnp.float32) + gate.astype(jnp.float32)[None, :] * total
-    ).astype(jnp.bfloat16)
+    ready = lax.optimization_barrier(residual.astype(jnp.float32) + gate_row * total)
+    return (ready + gate_row * from_x.astype(jnp.float32)).astype(jnp.bfloat16)
 
 
 def solution(mesh):

time: 131 us -> 129 us (0.985)
  waiting for transfers between devices: 50.9 us -> 46.9 us
    ppermute x14, waiting for transfers between devices: 20.2 us -> 16.6 us  [move_z(): return lax.ppermute(array, 'z', [(z, (z + step) % NZ) for z in range(NZ)])]
    all_to_all x1, waiting for transfers between devices: 0.01 us -> 2.64 us  [shards(): around = lax.all_to_all(stacked, 'y', 0, 0)]
    all_to_all x1, waiting for transfers between devices: 22.4 us -> 20.7 us  [shards(): returned = [lax.all_to_all(partials, ('y', 'x_lo'), 0, 0)]]
    ppermute x1, starting transfers between devices: 5.28 us -> 6.97 us  [shards(): from_core = lax.ppermute(for_core, 'core', swap).astype(jnp.float32)]
    add x0 -> x1, other arithmetic: none -> 1.36 us  [shards(): residual.astype(jnp.float32) + gate_row * total]
    ppermute x1, waiting for transfers between devices: 8.29 us -> 6.93 us  [shards(): from_x = lax.ppermute(chip_sum, 'x_hi', swap)]
    convert_element_type x2, other arithmetic: 2.22 us -> 0.89 us  [the longest x1 0.89 us: shards(): return (ready + gate_row * from_x.astype(jnp.float32)).astype(jnp.bfloat16)]
    pallas_call x1 -> x2, Pallas kernels: 19.4 us -> 20.5 us  [the longest x1 19.4 us: attend(): pl.pallas_call(functools.partial(attend_kernel, groups, 2 * count, heads[...]
  transfers between devices with their start and end apart: 20 -> 20, of which waited for: 11 -> 9; matrix products, arithmetic and copies ran while one was open for 1% -> 2% of each run, Pallas kernels for 7% -> 8%
where the time goes in v3:
time: 129 us; the launch traced here: 128 us
  waiting for transfers between devices  46.9 us (36%)
  starting transfers between devices  38.9 us (30%)
  Pallas kernels  34.3 us (27%)
  other arithmetic  4.82 us (4%)
  local copies, waits for them, and re-layouts  3.35 us (3%)
    all_to_all x1, waiting for transfers between devices, shards(): returned = [lax.all_to_all(partials, ('y', 'x_lo'), 0, 0)]  20.7 us
    ppermute x14, starting transfers between devices, move_z(): return lax.ppermute(array, 'z', [(z, (z + step) % NZ) for z in range(NZ)])  20 us
    pallas_call x1, Pallas kernels, attend(): pl.pallas_call(functools.partial(attend_kernel, groups, 2 * count, heads[...  19.4 us
    ppermute x14, waiting for transfers between devices, move_z(): return lax.ppermute(array, 'z', [(z, (z + step) % NZ) for z in range(NZ)])  16.6 us
    ppermute x1, starting transfers between devices, shards(): from_core = lax.ppermute(for_core, 'core', swap).astype(jnp.float32)  6.97 us
    ppermute x1, waiting for transfers between devices, shards(): from_x = lax.ppermute(chip_sum, 'x_hi', swap)  6.93 us
    pallas_call x2, Pallas kernels, project(): pl.pallas_call(project_kernel, grid_spec=pltpu.PrefetchScalarGridSpec(num...  5.75 us
    pallas_call x1, Pallas kernels, combine(): pl.pallas_call(combine_kernel, in_specs=[pl.BlockSpec(memory_space=pltpu....  5.11 us
  transfers between devices with their start and end apart: 20, of which 9 were waited for; matrix products, arithmetic and copies ran while one was open for 2% of the time, Pallas kernels for 8%

profile of v3, /device:TPU:1, one launch (start us, length us, event | category | flops | bytes accessed | tf_op | source)
XLA Modules:
  0.0 128.4 jit_solution(11141282834484913540)
XLA Ops:
  0.0 2.5 %collective-permute-start = (bf16[192,640]{1,0:T(8,128)(2,1)}, bf16[192,640]{1,0:T(8,128)(2,1)S(1)}, u32[]{:S(2)}, u32[]{:S(2)}) collective-permute-start(bf16[192,640]{1,0:T(8,128)(2,1)} %refs_0_.1), channel_id=1, source_target_pairs={{0,4},{4,8},{8,12},{12,16},{16,20},{20,24},{24,28},{28,0},{1,5},{5... | collective-permute-start | bytes 737288 | tf_op jit(solution)/shard_map/ppermute | solution.py:320
  2.5 3.9 %collective-permute-start.4 = (bf16[192,640]{1,0:T(8,128)(2,1)}, bf16[192,640]{1,0:T(8,128)(2,1)S(1)}, u32[]{:S(2)}, u32[]{:S(2)}) collective-permute-start(bf16[192,640]{1,0:T(8,128)(2,1)} %refs_1_.1), channel_id=1, source_target_pairs={{0,28},{4,0},{8,4},{12,8},{16,12},{20,16},{24,20},{28,24},{1,29},{... | collective-permute-start | bytes 737288 | tf_op jit(solution)/shard_map/ppermute | solution.py:320
  6.4 5.9 %collective-permute-done.refs_2_ = bf16[192,640]{1,0:T(8,128)(2,1)S(1)} collective-permute-done((bf16[192,640]{1,0:T(8,128)(2,1)}, bf16[192,640]{1,0:T(8,128)(2,1)S(1)}, u32[]{:S(2)}, u32[]{:S(2)}) %collective-permute-start) | collective-permute-done | bytes 245792 | tf_op jit(solution)/shard_map/ppermute | solution.py:320
  12.3 2.7 %collective-permute-start.5 = (bf16[192,640]{1,0:T(8,128)(2,1)S(1)}, bf16[192,640]{1,0:T(8,128)(2,1)S(1)}, u32[]{:S(2)}, u32[]{:S(2)}) collective-permute-start(bf16[192,640]{1,0:T(8,128)(2,1)S(1)} %collective-permute-done.4.refs_9_), channel_id=1, source_target_pairs={{0,28},{4,0},{8,4},{12,8},{16,12},{20,16},{24,20},{28,24},{1,29},{... | collective-permute-start | bytes 737288 | tf_op jit(solution)/shard_map/ppermute | solution.py:320
  17.7 2.1 %collective-permute-done.1.refs_4_ = bf16[192,640]{1,0:T(8,128)(2,1)S(1)} collective-permute-done((bf16[192,640]{1,0:T(8,128)(2,1)S(1)}, bf16[192,640]{1,0:T(8,128)(2,1)S(1)}, u32[]{:S(2)}, u32[]{:S(2)}) %collective-permute-start.1) | collective-permute-done | bytes 245792 | tf_op jit(solution)/shard_map/ppermute | solution.py:320
  19.8 2.7 %collective-permute-start.6 = (bf16[192,640]{1,0:T(8,128)(2,1)S(1)}, bf16[192,640]{1,0:T(8,128)(2,1)}, u32[]{:S(2)}, u32[]{:S(2)}) collective-permute-start(bf16[192,640]{1,0:T(8,128)(2,1)S(1)} %collective-permute-done.5.refs_11_), channel_id=1, source_target_pairs={{0,28},{4,0},{8,4},{12,8},{16,12},{20,16},{24,20},{28,24},{1,29},{... | collective-permute-start | bytes 737288 | tf_op jit(solution)/shard_map/ppermute | solution.py:320
  23.1 2.9 %repeat.1 = bf16[4,384,640]{2,1,0:T(8,128)(2,1)} custom-call(bf16[192,640]{1,0:T(8,128)(2,1)} %query_ref.1, bf16[192,640]{1,0:T(8,128)(2,1)} %copy-done.3), custom_call_target="tpu_custom_call" | custom-call | tf_op jit(solution)/shard_map/repeat/pallas_call | solution.py:215
  26.0 4.2 %all-to-all-start = ((bf16[4,384,640]{2,1,0:T(8,128)(2,1)}), bf16[4,384,640]{2,1,0:T(8,128)(2,1)S(1)}, u32[]{:S(2)}, u32[]{:S(2)}) async-start(bf16[4,384,640]{2,1,0:T(8,128)(2,1)} %repeat.1), calls=%async_computation | async-start | bytes 3932160 | tf_op jit(solution)/shard_map/all_to_all | solution.py:335
  30.2 1.4 %collective-permute-start.13 = (bf16[192,640]{1,0:T(8,128)(2,1)S(1)}, bf16[192,640]{1,0:T(8,128)(2,1)}, u32[]{:S(2)}, u32[]{:S(2)}) collective-permute-start(bf16[192,640]{1,0:T(8,128)(2,1)S(1)} %collective-permute-done.9.refs_8_), channel_id=1, source_target_pairs={{0,28},{4,0},{8,4},{12,8},{16,12},{20,16},{24,20},{28,24},{1,29},{... | collective-permute-start | bytes 737288 | tf_op jit(solution)/shard_map/ppermute | solution.py:320
  31.7 2.6 %collective-permute-start.7 = (bf16[192,640]{1,0:T(8,128)(2,1)}, bf16[192,640]{1,0:T(8,128)(2,1)}, u32[]{:S(2)}, u32[]{:S(2)}) collective-permute-start(bf16[192,640]{1,0:T(8,128)(2,1)} %collective-permute-done.6.refs_13_), channel_id=1, source_target_pairs={{0,28},{4,0},{8,4},{12,8},{16,12},{20,16},{24,20},{28,24},{1,29},{... | collective-permute-start | bytes 737288 | tf_op jit(solution)/shard_map/ppermute | solution.py:320
  35.3 2.6 %collective-permute-start.14 = (bf16[192,640]{1,0:T(8,128)(2,1)}, bf16[192,640]{1,0:T(8,128)(2,1)}, u32[]{:S(2)}, u32[]{:S(2)}) collective-permute-start(bf16[192,640]{1,0:T(8,128)(2,1)} %collective-permute-done.13.refs_10_), channel_id=1, source_target_pairs={{0,28},{4,0},{8,4},{12,8},{16,12},{20,16},{24,20},{28,24},{1,29},{... | collective-permute-start | bytes 737288 | tf_op jit(solution)/shard_map/ppermute | solution.py:320
  38.0 2.8 %collective-permute-done.3.keys_ref.refs_14_ = bf16[192,640]{1,0:T(8,128)(2,1)} collective-permute-done((bf16[192,640]{1,0:T(8,128)(2,1)}, bf16[192,640]{1,0:T(8,128)(2,1)}, u32[]{:S(2)}, u32[]{:S(2)}) %collective-permute-start.3) | collective-permute-done | bytes 245792 | tf_op jit(solution)/shard_map/ppermute | solution.py:320
  42.0 2.1 %collective-permute-done.14.refs_12_ = bf16[192,640]{1,0:T(8,128)(2,1)} collective-permute-done((bf16[192,640]{1,0:T(8,128)(2,1)}, bf16[192,640]{1,0:T(8,128)(2,1)}, u32[]{:S(2)}, u32[]{:S(2)}) %collective-permute-start.14) | collective-permute-done | bytes 245792 | tf_op jit(solution)/shard_map/ppermute | solution.py:320
  44.1 3.4 %collective-permute-done.12.refs_7_ = bf16[192,640]{1,0:T(8,128)(2,1)} collective-permute-done((bf16[192,640]{1,0:T(8,128)(2,1)}, bf16[192,640]{1,0:T(8,128)(2,1)}, u32[]{:S(2)}, u32[]{:S(2)}) %collective-permute-start.12) | collective-permute-done | bytes 245792 | tf_op jit(solution)/shard_map/ppermute | solution.py:320
  47.5 2.6 %all-to-all-done.around_ref = bf16[4,384,640]{2,1,0:T(8,128)(2,1)S(1)} async-done(((bf16[4,384,640]{2,1,0:T(8,128)(2,1)}), bf16[4,384,640]{2,1,0:T(8,128)(2,1)S(1)}, u32[]{:S(2)}, u32[]{:S(2)}) %all-to-all-start) | async-done | bytes 1966112 | tf_op jit(solution)/shard_map/all_to_all | solution.py:335
  51.4 19.4 %attend.1 = bf16[8,208,640]{2,1,0:T(8,128)(2,1)} custom-call(s32[2]{0:T(128)} %last_of.1.place_ref, bf16[192,640]{1,0:T(8,128)(2,1)} %query_ref.1, bf16[4,384,640]{2,1,0:T(8,128)(2,1)} %copy-done.1, bf16[192,640]{1,0:T(8,128)(2,1)} %refs_0_.1, bf16[192,640]{1,0:T(8,128)(2,1)} %refs_1_.1, bf16[192,640]{1,0:T(8,128)(2,1)} %copy-done.6, ...), custom_call_target="tpu_custom_call" | custom-call | flops 24159191040 | tf_op jit(solution)/shard_map/attend/pallas_call | solution.py:162
  70.7 3.6 %all-to-all-start.1 = ((bf16[8,208,640]{2,1,0:T(8,128)(2,1)}), bf16[8,208,640]{2,1,0:T(8,128)(2,1)S(1)}, u32[]{:S(2)}, u32[]{:S(2)}) async-start(bf16[8,208,640]{2,1,0:T(8,128)(2,1)} %attend.1), calls=%async_computation.1 | async-start | bytes 4259840 | tf_op jit(solution)/shard_map/all_to_all | solution.py:350
  75.0 20.7 %all-to-all-done.1.refs_0_ = bf16[8,208,640]{2,1,0:T(8,128)(2,1)S(1)} async-done(((bf16[8,208,640]{2,1,0:T(8,128)(2,1)}), bf16[8,208,640]{2,1,0:T(8,128)(2,1)S(1)}, u32[]{:S(2)}, u32[]{:S(2)}) %all-to-all-start.1) | async-done | bytes 2129952 | tf_op jit(solution)/shard_map/all_to_all | solution.py:350
  97.1 5.1 %combine.1 = (bf16[192,640]{1,0:T(8,128)(2,1)}, bf16[192,1280]{1,0:T(8,128)(2,1)}, bf16[192,1280]{1,0:T(8,128)(2,1)}) custom-call(s32[2]{0:T(128)} %pad_add_fusion.blocks_ref, bf16[640,5120]{1,0:T(8,128)(2,1)} %w_ref.5, bf16[8,208,640]{2,1,0:T(8,128)(2,1)} %copy-done), custom_call_target="tpu_custom_call" | custom-call | tf_op jit(solution)/shard_map/combine/pallas_call | solution.py:270
  102.2 7.0 %collective-permute-start.15 = (bf16[192,1280]{1,0:T(8,128)(2,1)}, bf16[192,1280]{1,0:T(8,128)(2,1)S(1)}, u32[]{:S(2)}, u32[]{:S(2)}) collective-permute-start(bf16[192,1280]{1,0:T(8,128)(2,1)} %get-tuple-element.14), channel_id=1, source_target_pairs={{0,1},{1,0},{2,3},{3,2},{4,5},{5,4},{6,7},{7,6},{8,9},{9,8},{10,11... | collective-permute-start | bytes 1474568 | tf_op jit(solution)/shard_map/ppermute | solution.py:361
  109.2 2.9 %project.2 = f32[192,1280]{1,0:T(8,128)} custom-call(s32[1]{0:T(128)} %bitcast.5.block_ref, bf16[192,640]{1,0:T(8,128)(2,1)} %get-tuple-element.15.a_ref, bf16[640,5120]{1,0:T(8,128)(2,1)} %w_ref.5), custom_call_target="tpu_custom_call" | custom-call | tf_op jit(solution)/shard_map/project/pallas_call | solution.py:302
  113.5 2.8 %collective-permute-start.17 = (bf16[192,1280]{1,0:T(8,128)(2,1)S(1)}, bf16[192,1280]{1,0:T(8,128)(2,1)S(1)}, u32[]{:S(2)}, u32[]{:S(2)}) collective-permute-start(bf16[192,1280]{1,0:T(8,128)(2,1)S(1)} %add_convert_fusion.1), channel_id=1, source_target_pairs={{0,2},{2,0},{1,3},{3,1},{4,6},{6,4},{5,7},{7,5},{8,10},{10,8},{9,1... | collective-permute-start | bytes 1474568 | tf_op jit(solution)/shard_map/ppermute | solution.py:364
  116.3 2.9 %project.3 = f32[192,1280]{1,0:T(8,128)} custom-call(s32[1]{0:T(128)} %bitcast.block_ref, bf16[192,640]{1,0:T(8,128)(2,1)} %get-tuple-element.15.a_ref, bf16[640,5120]{1,0:T(8,128)(2,1)} %w_ref.5), custom_call_target="tpu_custom_call" | custom-call | tf_op jit(solution)/shard_map/project/pallas_call | solution.py:302
  120.6 6.9 %collective-permute-done.17 = bf16[192,1280]{1,0:T(8,128)(2,1)S(1)} collective-permute-done((bf16[192,1280]{1,0:T(8,128)(2,1)S(1)}, bf16[192,1280]{1,0:T(8,128)(2,1)S(1)}, u32[]{:S(2)}, u32[]{:S(2)}) %collective-permute-start.17) | collective-permute-done | bytes 491552 | tf_op jit(solution)/shard_map/ppermute | solution.py:364
  (52 shorter events, 12.7 us)
Async XLA Ops:
  0.0 12.3 %collective-permute-start = (bf16[192,640]{1,0:T(8,128)(2,1)}, bf16[192,640]{1,0:T(8,128)(2,1)S(1)}, u32[]{:S(2)}, u32[]{:S(2)}) collective-permute-start(bf16[192,640]{1,0:T(8,128)(2,1)} %refs_0_.1), channel_id=1, source_target_pairs={{0,4},{4,8},{8,12},{12,16},{16,20},{20,24},{24,28},{28,0},{1,5},{5... | collective-permute-start | bytes 737288 | tf_op jit(solution)/shard_map/ppermute | solution.py:320
  2.5 9.8 %collective-permute-start.4 = (bf16[192,640]{1,0:T(8,128)(2,1)}, bf16[192,640]{1,0:T(8,128)(2,1)S(1)}, u32[]{:S(2)}, u32[]{:S(2)}) collective-permute-start(bf16[192,640]{1,0:T(8,128)(2,1)} %refs_1_.1), channel_id=1, source_target_pairs={{0,28},{4,0},{8,4},{12,8},{16,12},{20,16},{24,20},{28,24},{1,29},{... | collective-permute-start | bytes 737288 | tf_op jit(solution)/shard_map/ppermute | solution.py:320
  12.3 29.7 %copy-start.6 = (bf16[192,640]{1,0:T(8,128)(2,1)}, bf16[192,640]{1,0:T(8,128)(2,1)S(1)}, u32[]{:S(2)}) copy-start(bf16[192,640]{1,0:T(8,128)(2,1)S(1)} %collective-permute-done.refs_2_) | copy-start | bytes 737284
  12.3 7.4 %collective-permute-start.1 = (bf16[192,640]{1,0:T(8,128)(2,1)S(1)}, bf16[192,640]{1,0:T(8,128)(2,1)S(1)}, u32[]{:S(2)}, u32[]{:S(2)}) collective-permute-start(bf16[192,640]{1,0:T(8,128)(2,1)S(1)} %collective-permute-done.refs_2_), channel_id=1, source_target_pairs={{0,4},{4,8},{8,12},{12,16},{16,20},{20,24},{24,28},{28,0},{1,5},{5... | collective-permute-start | bytes 737288 | tf_op jit(solution)/shard_map/ppermute | solution.py:320
  12.3 29.7 %copy-start.7 = (bf16[192,640]{1,0:T(8,128)(2,1)}, bf16[192,640]{1,0:T(8,128)(2,1)S(1)}, u32[]{:S(2)}) copy-start(bf16[192,640]{1,0:T(8,128)(2,1)S(1)} %collective-permute-done.4.refs_9_) | copy-start | bytes 737284
  12.3 7.4 %collective-permute-start.5 = (bf16[192,640]{1,0:T(8,128)(2,1)S(1)}, bf16[192,640]{1,0:T(8,128)(2,1)S(1)}, u32[]{:S(2)}, u32[]{:S(2)}) collective-permute-start(bf16[192,640]{1,0:T(8,128)(2,1)S(1)} %collective-permute-done.4.refs_9_), channel_id=1, source_target_pairs={{0,28},{4,0},{8,4},{12,8},{16,12},{20,16},{24,20},{28,24},{1,29},{... | collective-permute-start | bytes 737288 | tf_op jit(solution)/shard_map/ppermute | solution.py:320
  15.0 7.4 %collective-permute-start.8 = (bf16[192,640]{1,0:T(8,128)(2,1)}, bf16[192,640]{1,0:T(8,128)(2,1)S(1)}, u32[]{:S(2)}, u32[]{:S(2)}) collective-permute-start(bf16[192,640]{1,0:T(8,128)(2,1)} %query_ref.1), channel_id=1, source_target_pairs={{0,32},{32,0},{1,33},{33,1},{2,34},{34,2},{3,35},{35,3},{4,36},{36... | collective-permute-start | bytes 737288 | tf_op jit(solution)/shard_map/ppermute | solution.py:328
  16.2 9.8 %collective-permute-start.9 = (bf16[192,640]{1,0:T(8,128)(2,1)}, bf16[192,640]{1,0:T(8,128)(2,1)S(1)}, u32[]{:S(2)}, u32[]{:S(2)}) collective-permute-start(bf16[192,640]{1,0:T(8,128)(2,1)} %refs_0_.1), channel_id=1, source_target_pairs={{0,28},{4,0},{8,4},{12,8},{16,12},{20,16},{24,20},{28,24},{1,29},{... | collective-permute-start | bytes 737288 | tf_op jit(solution)/shard_map/ppermute | solution.py:320
  16.3 15.3 %collective-permute-start.10 = (bf16[192,640]{1,0:T(8,128)(2,1)}, bf16[192,640]{1,0:T(8,128)(2,1)S(1)}, u32[]{:S(2)}, u32[]{:S(2)}) collective-permute-start(bf16[192,640]{1,0:T(8,128)(2,1)} %refs_1_.1), channel_id=1, source_target_pairs={{0,4},{4,8},{8,12},{12,16},{16,20},{20,24},{24,28},{28,0},{1,5},{5... | collective-permute-start | bytes 737288 | tf_op jit(solution)/shard_map/ppermute | solution.py:320
  19.7 22.3 %copy-start.8 = (bf16[192,640]{1,0:T(8,128)(2,1)}, bf16[192,640]{1,0:T(8,128)(2,1)S(1)}, u32[]{:S(2)}) copy-start(bf16[192,640]{1,0:T(8,128)(2,1)S(1)} %collective-permute-done.1.refs_4_) | copy-start | bytes 737284
  19.7 11.9 %collective-permute-start.2 = (bf16[192,640]{1,0:T(8,128)(2,1)S(1)}, bf16[192,640]{1,0:T(8,128)(2,1)}, u32[]{:S(2)}, u32[]{:S(2)}) collective-permute-start(bf16[192,640]{1,0:T(8,128)(2,1)S(1)} %collective-permute-done.1.refs_4_), channel_id=1, source_target_pairs={{0,4},{4,8},{8,12},{12,16},{16,20},{20,24},{24,28},{28,0},{1,5},{5... | collective-permute-start | bytes 737288 | tf_op jit(solution)/shard_map/ppermute | solution.py:320
  19.7 22.3 %copy-start.9 = (bf16[192,640]{1,0:T(8,128)(2,1)}, bf16[192,640]{1,0:T(8,128)(2,1)S(1)}, u32[]{:S(2)}) copy-start(bf16[192,640]{1,0:T(8,128)(2,1)S(1)} %collective-permute-done.5.refs_11_) | copy-start | bytes 737284
  19.8 12.0 %collective-permute-start.6 = (bf16[192,640]{1,0:T(8,128)(2,1)S(1)}, bf16[192,640]{1,0:T(8,128)(2,1)}, u32[]{:S(2)}, u32[]{:S(2)}) collective-permute-start(bf16[192,640]{1,0:T(8,128)(2,1)S(1)} %collective-permute-done.5.refs_11_), channel_id=1, source_target_pairs={{0,28},{4,0},{8,4},{12,8},{16,12},{20,16},{24,20},{28,24},{1,29},{... | collective-permute-start | bytes 737288 | tf_op jit(solution)/shard_map/ppermute | solution.py:320
  26.0 24.1 %all-to-all-start = ((bf16[4,384,640]{2,1,0:T(8,128)(2,1)}), bf16[4,384,640]{2,1,0:T(8,128)(2,1)S(1)}, u32[]{:S(2)}, u32[]{:S(2)}) async-start(bf16[4,384,640]{2,1,0:T(8,128)(2,1)} %repeat.1), calls=%async_computation | async-start | bytes 3932160 | tf_op jit(solution)/shard_map/all_to_all | solution.py:335
  30.2 5.2 %collective-permute-start.13 = (bf16[192,640]{1,0:T(8,128)(2,1)S(1)}, bf16[192,640]{1,0:T(8,128)(2,1)}, u32[]{:S(2)}, u32[]{:S(2)}) collective-permute-start(bf16[192,640]{1,0:T(8,128)(2,1)S(1)} %collective-permute-done.9.refs_8_), channel_id=1, source_target_pairs={{0,28},{4,0},{8,4},{12,8},{16,12},{20,16},{24,20},{28,24},{1,29},{... | collective-permute-start | bytes 737288 | tf_op jit(solution)/shard_map/ppermute | solution.py:320
  31.6 6.4 %collective-permute-start.11 = (bf16[192,640]{1,0:T(8,128)(2,1)S(1)}, bf16[192,640]{1,0:T(8,128)(2,1)}, u32[]{:S(2)}, u32[]{:S(2)}) collective-permute-start(bf16[192,640]{1,0:T(8,128)(2,1)S(1)} %collective-permute-done.10.refs_3_), channel_id=1, source_target_pairs={{0,4},{4,8},{8,12},{12,16},{16,20},{20,24},{24,28},{28,0},{1,5},{5... | collective-permute-start | bytes 737288 | tf_op jit(solution)/shard_map/ppermute | solution.py:320
  31.7 9.1 %collective-permute-start.3 = (bf16[192,640]{1,0:T(8,128)(2,1)}, bf16[192,640]{1,0:T(8,128)(2,1)}, u32[]{:S(2)}, u32[]{:S(2)}) collective-permute-start(bf16[192,640]{1,0:T(8,128)(2,1)} %collective-permute-done.2.refs_6_), channel_id=1, source_target_pairs={{0,4},{4,8},{8,12},{12,16},{16,20},{20,24},{24,28},{28,0},{1,5},{5... | collective-permute-start | bytes 737288 | tf_op jit(solution)/shard_map/ppermute | solution.py:320
  31.7 9.0 %collective-permute-start.7 = (bf16[192,640]{1,0:T(8,128)(2,1)}, bf16[192,640]{1,0:T(8,128)(2,1)}, u32[]{:S(2)}, u32[]{:S(2)}) collective-permute-start(bf16[192,640]{1,0:T(8,128)(2,1)} %collective-permute-done.6.refs_13_), channel_id=1, source_target_pairs={{0,28},{4,0},{8,4},{12,8},{16,12},{20,16},{24,20},{28,24},{1,29},{... | collective-permute-start | bytes 737288 | tf_op jit(solution)/shard_map/ppermute | solution.py:320
  35.3 8.8 %collective-permute-start.14 = (bf16[192,640]{1,0:T(8,128)(2,1)}, bf16[192,640]{1,0:T(8,128)(2,1)}, u32[]{:S(2)}, u32[]{:S(2)}) collective-permute-start(bf16[192,640]{1,0:T(8,128)(2,1)} %collective-permute-done.13.refs_10_), channel_id=1, source_target_pairs={{0,28},{4,0},{8,4},{12,8},{16,12},{20,16},{24,20},{28,24},{1,29},{... | collective-permute-start | bytes 737288 | tf_op jit(solution)/shard_map/ppermute | solution.py:320
  38.0 9.5 %collective-permute-start.12 = (bf16[192,640]{1,0:T(8,128)(2,1)}, bf16[192,640]{1,0:T(8,128)(2,1)}, u32[]{:S(2)}, u32[]{:S(2)}) collective-permute-start(bf16[192,640]{1,0:T(8,128)(2,1)} %collective-permute-done.11.refs_5_), channel_id=1, source_target_pairs={{0,4},{4,8},{8,12},{12,16},{16,20},{20,24},{24,28},{28,0},{1,5},{5... | collective-permute-start | bytes 737288 | tf_op jit(solution)/shard_map/ppermute | solution.py:320
  70.7 25.0 %all-to-all-start.1 = ((bf16[8,208,640]{2,1,0:T(8,128)(2,1)}), bf16[8,208,640]{2,1,0:T(8,128)(2,1)S(1)}, u32[]{:S(2)}, u32[]{:S(2)}) async-start(bf16[8,208,640]{2,1,0:T(8,128)(2,1)} %attend.1), calls=%async_computation.1 | async-start | bytes 4259840 | tf_op jit(solution)/shard_map/all_to_all | solution.py:350
  102.2 9.8 %collective-permute-start.15 = (bf16[192,1280]{1,0:T(8,128)(2,1)}, bf16[192,1280]{1,0:T(8,128)(2,1)S(1)}, u32[]{:S(2)}, u32[]{:S(2)}) collective-permute-start(bf16[192,1280]{1,0:T(8,128)(2,1)} %get-tuple-element.14), channel_id=1, source_target_pairs={{0,1},{1,0},{2,3},{3,2},{4,5},{5,4},{6,7},{7,6},{8,9},{9,8},{10,11... | collective-permute-start | bytes 1474568 | tf_op jit(solution)/shard_map/ppermute | solution.py:361
  113.4 5.8 %collective-permute-start.16 = (bf16[192,1280]{1,0:T(8,128)(2,1)S(1)}, bf16[192,1280]{1,0:T(8,128)(2,1)S(1)}, u32[]{:S(2)}, u32[]{:S(2)}) collective-permute-start(bf16[192,1280]{1,0:T(8,128)(2,1)S(1)} %copy-done.5), channel_id=1, source_target_pairs={{0,1},{1,0},{2,3},{3,2},{4,5},{5,4},{6,7},{7,6},{8,9},{9,8},{10,11... | collective-permute-start | bytes 1474568 | tf_op jit(solution)/shard_map/ppermute | solution.py:366
  113.5 14.0 %collective-permute-start.17 = (bf16[192,1280]{1,0:T(8,128)(2,1)S(1)}, bf16[192,1280]{1,0:T(8,128)(2,1)S(1)}, u32[]{:S(2)}, u32[]{:S(2)}) collective-permute-start(bf16[192,1280]{1,0:T(8,128)(2,1)S(1)} %add_convert_fusion.1), channel_id=1, source_target_pairs={{0,2},{2,0},{1,3},{3,1},{4,6},{6,4},{5,7},{7,5},{8,10},{10,8},{9,1... | collective-permute-start | bytes 1474568 | tf_op jit(solution)/shard_map/ppermute | solution.py:364
  (8 other events, 41.1 us)

commit v4 on v3

--- a/solution.py
+++ b/solution.py
@@ -12,7 +12,7 @@
 EXP2_SCALE = HD ** (-0.5) * math.log2(math.e)
 NY, NX, NZ = 4, 2, 8
 STAT_ROWS = 16
-BIG = 60
+BIG, SMALL = 60, 16
 OFFSETS = [(dy, dx) for dy in range(NY) for dx in range(NX)]
 
 
@@ -223,16 +223,16 @@
     )(a, b)
 
 
-def combine_kernel(blocks_ref, w_ref, *refs):
-    *parts_refs, out_ref, first_ref, second_ref, w_buf, sems = refs
-    product_refs = (first_ref, second_ref)
-    columns = first_ref.shape[1]
-    copies = []
-    for i in range(len(product_refs)):
-        first = pl.multiple_of(blocks_ref[i] * columns, columns)
-        copy = pltpu.make_async_copy(w_ref.at[:, pl.ds(first, columns)], w_buf.at[i], sems.at[i])
-        copy.start()
-        copies.append(copy)
+def multiply_out(a_ref, w_ref, out_ref):
+    for first in range(0, out_ref.shape[1], 2 * HD):
+        columns = slice(first, first + 2 * HD)
+        out_ref[:, columns] = jnp.dot(
+            a_ref[...], w_ref[:, columns], preferred_element_type=jnp.float32
+        ).astype(out_ref.dtype)
+
+
+def combine_kernel(w_ref, *refs):
+    *parts_refs, out_ref, first_ref, second_ref = refs
     group = parts_refs[0].shape[0]
     rows, width = out_ref.shape
     heads = width // HD
@@ -256,43 +256,47 @@
             mixture = parts_ref[part, :rows, columns].astype(jnp.float32)
             total = total + by_row[:, at : at + 1] * mixture
         out_ref[:, head_columns(head)] = total.astype(jnp.bfloat16)
-    for i, product_ref in enumerate(product_refs):
-        copies[i].wait()
-        product_ref[...] = jnp.dot(
-            out_ref[...], w_buf[i], preferred_element_type=jnp.float32
-        ).astype(jnp.bfloat16)
-
-
-def combine(blocks, parts, out_weight, columns):
+    for i, product_ref in enumerate((first_ref, second_ref)):
+        multiply_out(out_ref, w_ref.at[i], product_ref)
+
+
+def combine(weights, parts):
     rows = parts[0].shape[1] - STAT_ROWS
-    width = sum(part.shape[2] for part in parts)
-    vmem = pl.BlockSpec(memory_space=pltpu.VMEM)
+    _, width, columns = weights.shape
     return pl.pallas_call(
         combine_kernel,
-        in_specs=[
-            pl.BlockSpec(memory_space=pltpu.SMEM),
-            pl.BlockSpec(memory_space=pl.ANY),
-            *[vmem] * len(parts),
-        ],
-        out_specs=[vmem, vmem, vmem],
         out_shape=[
             jax.ShapeDtypeStruct((rows, width), jnp.bfloat16),
             jax.ShapeDtypeStruct((rows, columns), jnp.bfloat16),
             jax.ShapeDtypeStruct((rows, columns), jnp.bfloat16),
         ],
-        scratch_shapes=[
-            pltpu.VMEM((2, width, columns), jnp.bfloat16),
-            pltpu.SemaphoreType.DMA((2,)),
-        ],
-        compiler_params=pltpu.CompilerParams(vmem_limit_bytes=BIG * 2**20),
+        compiler_params=pltpu.CompilerParams(vmem_limit_bytes=SMALL * 2**20),
         name="combine",
-    )(blocks, out_weight, *parts)
+    )(weights, *parts)
+
+
+def select_kernel(block_ref, w_ref, out_ref):
+    out_ref[...] = w_ref[...]
+
+
+def select_columns(blocks, weight, columns):
+    rows, count = weight.shape[0], blocks.shape[0]
+    return pl.pallas_call(
+        select_kernel,
+        grid_spec=pltpu.PrefetchScalarGridSpec(
+            num_scalar_prefetch=1,
+            grid=(count,),
+            in_specs=[pl.BlockSpec((rows, columns), lambda i, block: (0, block[i]))],
+            out_specs=pl.BlockSpec((None, rows, columns), lambda i, block: (i, 0, 0)),
+        ),
+        out_shape=jax.ShapeDtypeStruct((count, rows, columns), weight.dtype),
+        compiler_params=pltpu.CompilerParams(vmem_limit_bytes=SMALL * 2**20),
+        name="select_columns",
+    )(blocks, weight)
 
 
 def project_kernel(block_ref, a_ref, w_ref, out_ref):
-    out_ref[...] = jnp.dot(
-        a_ref[...], w_ref[...], preferred_element_type=jnp.float32
-    ).astype(out_ref.dtype)
+    multiply_out(a_ref, w_ref, out_ref)
 
 
 def project(block, attended, out_weight, columns, dtype):
@@ -311,7 +315,7 @@
             out_specs=pl.BlockSpec((rows, part), lambda i, block: (0, i)),
         ),
         out_shape=jax.ShapeDtypeStruct((rows, columns), dtype),
-        compiler_params=pltpu.CompilerParams(vmem_limit_bytes=BIG * 2**20),
+        compiler_params=pltpu.CompilerParams(vmem_limit_bytes=SMALL * 2**20),
         name="project",
     )(block, attended, out_weight)
 
@@ -352,14 +356,14 @@
     def block(x_half, core_half):
         return (x_half * 2 + core_half).astype(jnp.int32).reshape(1)
 
+    both = jnp.concatenate([block(1 - x_hi, 1 - core), block(x_hi, 1 - core)])
+    both, own_block, _ = lax.optimization_barrier((both, block(1 - x_hi, core), partials))
+    own_weight = select_columns(own_block, out_weight, columns)[0]
     attended, for_core, for_core_late = combine(
-        jnp.concatenate([block(1 - x_hi, 1 - core), block(x_hi, 1 - core)]),
-        returned,
-        out_weight,
-        columns,
+        select_columns(both, out_weight, columns), returned
     )
     from_core = lax.ppermute(for_core, "core", swap).astype(jnp.float32)
-    chip_sum = project(block(1 - x_hi, core), attended, out_weight, columns, jnp.float32)
+    chip_sum = project(jnp.zeros_like(own_block), attended, own_weight, columns, jnp.float32)
     chip_sum = (chip_sum + from_core).astype(jnp.bfloat16)
     from_x = lax.ppermute(chip_sum, "x_hi", swap)
     attended, for_core_late, _ = lax.optimization_barrier((attended, for_core_late, chip_sum))

time: 129 us -> 128 us (level)
  local copies, waits for them, and re-layouts: 3.35 us -> 10.6 us
  waiting for transfers between devices: 46.9 us -> 42.4 us
  other arithmetic: 4.82 us -> 1.87 us
  Pallas kernels: 34.3 us -> 31.5 us
  starting transfers between devices: 38.9 us -> 40.9 us
    unnamed x24 -> x26, local copies, waits for them, and re-layouts: 3.35 us -> 10.6 us
    pallas_call x2, Pallas kernels: 5.75 us -> 2.13 us  [project(): pl.pallas_call(project_kernel, grid_spec=pltpu.PrefetchScalarGridSpec(num...]
    all_to_all x1, waiting for transfers between devices: 20.7 us -> 17.5 us  [shards(): returned = [lax.all_to_all(partials, ('y', 'x_lo'), 0, 0)]]
    ppermute x14, waiting for transfers between devices: 16.6 us -> 14 us  [move_z(): return lax.ppermute(array, 'z', [(z, (z + step) % NZ) for z in range(NZ)])]
    ppermute x14, starting transfers between devices: 20 us -> 21.3 us  [move_z(): return lax.ppermute(array, 'z', [(z, (z + step) % NZ) for z in range(NZ)])]
    pallas_call x1 -> x3, Pallas kernels: 5.11 us -> 5.91 us  [the longest x1 4.76 us: combine(): pl.pallas_call(combine_kernel, out_shape=[jax.ShapeDtypeStruct((rows, wid...]
  transfers between devices with their start and end apart: 20 -> 20, of which waited for: 9 -> 8; matrix products, arithmetic and copies ran while one was open for 2% -> 1% of each run, Pallas kernels for 8% -> 6%
where the time goes in v4:
time: 128 us; the launch traced here: 127 us
  waiting for transfers between devices  42.4 us (33%)
  starting transfers between devices  40.9 us (32%)
  Pallas kernels  31.5 us (25%)
  local copies, waits for them, and re-layouts  10.6 us (8%)
  other arithmetic  1.87 us (1%)
    ppermute x14, starting transfers between devices, move_z(): return lax.ppermute(array, 'z', [(z, (z + step) % NZ) for z in range(NZ)])  21.3 us
    pallas_call x1, Pallas kernels, attend(): pl.pallas_call(functools.partial(attend_kernel, groups, 2 * count, heads[...  19.4 us
    all_to_all x1, waiting for transfers between devices, shards(): returned = [lax.all_to_all(partials, ('y', 'x_lo'), 0, 0)]  17.5 us
    ppermute x14, waiting for transfers between devices, move_z(): return lax.ppermute(array, 'z', [(z, (z + step) % NZ) for z in range(NZ)])  14 us
    unnamed x26, local copies, waits for them, and re-layouts  10.6 us
    ppermute x1, waiting for transfers between devices, shards(): from_x = lax.ppermute(chip_sum, 'x_hi', swap)  7.02 us
    ppermute x1, starting transfers between devices, shards(): from_core = lax.ppermute(for_core, 'core', swap).astype(jnp.float32)  6.89 us
    pallas_call x1, Pallas kernels, combine(): pl.pallas_call(combine_kernel, out_shape=[jax.ShapeDtypeStruct((rows, wid...  4.76 us
  transfers between devices with their start and end apart: 20, of which 8 were waited for; matrix products, arithmetic and copies ran while one was open for 1% of the time, Pallas kernels for 6%

profile of v4, /device:TPU:1, one launch (start us, length us, event | category | flops | bytes accessed | tf_op | source)
XLA Modules:
  0.0 127.4 jit_solution(3636660866349649689)
XLA Ops:
  0.0 2.5 %collective-permute-start = (bf16[192,640]{1,0:T(8,128)(2,1)}, bf16[192,640]{1,0:T(8,128)(2,1)S(1)}, u32[]{:S(2)}, u32[]{:S(2)}) collective-permute-start(bf16[192,640]{1,0:T(8,128)(2,1)} %refs_0_.1), channel_id=1, source_target_pairs={{0,4},{4,8},{8,12},{12,16},{16,20},{20,24},{24,28},{28,0},{1,5},{5... | collective-permute-start | bytes 737288 | tf_op jit(solution)/shard_map/ppermute | solution.py:324
  2.5 3.9 %collective-permute-start.4 = (bf16[192,640]{1,0:T(8,128)(2,1)}, bf16[192,640]{1,0:T(8,128)(2,1)S(1)}, u32[]{:S(2)}, u32[]{:S(2)}) collective-permute-start(bf16[192,640]{1,0:T(8,128)(2,1)} %refs_1_.1), channel_id=1, source_target_pairs={{0,28},{4,0},{8,4},{12,8},{16,12},{20,16},{24,20},{28,24},{1,29},{... | collective-permute-start | bytes 737288 | tf_op jit(solution)/shard_map/ppermute | solution.py:324
  6.4 5.9 %collective-permute-done.refs_2_ = bf16[192,640]{1,0:T(8,128)(2,1)S(1)} collective-permute-done((bf16[192,640]{1,0:T(8,128)(2,1)}, bf16[192,640]{1,0:T(8,128)(2,1)S(1)}, u32[]{:S(2)}, u32[]{:S(2)}) %collective-permute-start) | collective-permute-done | bytes 245792 | tf_op jit(solution)/shard_map/ppermute | solution.py:324
  12.3 2.7 %collective-permute-start.5 = (bf16[192,640]{1,0:T(8,128)(2,1)S(1)}, bf16[192,640]{1,0:T(8,128)(2,1)S(1)}, u32[]{:S(2)}, u32[]{:S(2)}) collective-permute-start(bf16[192,640]{1,0:T(8,128)(2,1)S(1)} %collective-permute-done.4.refs_9_), channel_id=1, source_target_pairs={{0,28},{4,0},{8,4},{12,8},{16,12},{20,16},{24,20},{28,24},{1,29},{... | collective-permute-start | bytes 737288 | tf_op jit(solution)/shard_map/ppermute | solution.py:324
  16.3 1.4 %collective-permute-start.10 = (bf16[192,640]{1,0:T(8,128)(2,1)}, bf16[192,640]{1,0:T(8,128)(2,1)S(1)}, u32[]{:S(2)}, u32[]{:S(2)}) collective-permute-start(bf16[192,640]{1,0:T(8,128)(2,1)} %refs_1_.1), channel_id=1, source_target_pairs={{0,4},{4,8},{8,12},{12,16},{16,20},{20,24},{24,28},{28,0},{1,5},{5... | collective-permute-start | bytes 737288 | tf_op jit(solution)/shard_map/ppermute | solution.py:324
  17.7 2.1 %collective-permute-done.1.refs_4_ = bf16[192,640]{1,0:T(8,128)(2,1)S(1)} collective-permute-done((bf16[192,640]{1,0:T(8,128)(2,1)S(1)}, bf16[192,640]{1,0:T(8,128)(2,1)S(1)}, u32[]{:S(2)}, u32[]{:S(2)}) %collective-permute-start.1) | collective-permute-done | bytes 245792 | tf_op jit(solution)/shard_map/ppermute | solution.py:324
  19.8 2.7 %collective-permute-start.6 = (bf16[192,640]{1,0:T(8,128)(2,1)S(1)}, bf16[192,640]{1,0:T(8,128)(2,1)}, u32[]{:S(2)}, u32[]{:S(2)}) collective-permute-start(bf16[192,640]{1,0:T(8,128)(2,1)S(1)} %collective-permute-done.5.refs_11_), channel_id=1, source_target_pairs={{0,28},{4,0},{8,4},{12,8},{16,12},{20,16},{24,20},{28,24},{1,29},{... | collective-permute-start | bytes 737288 | tf_op jit(solution)/shard_map/ppermute | solution.py:324
  23.1 2.9 %repeat.1 = bf16[4,384,640]{2,1,0:T(8,128)(2,1)} custom-call(bf16[192,640]{1,0:T(8,128)(2,1)} %query_ref.1, bf16[192,640]{1,0:T(8,128)(2,1)} %copy-done.5), custom_call_target="tpu_custom_call" | custom-call | tf_op jit(solution)/shard_map/repeat/pallas_call | solution.py:215
  26.0 4.2 %all-to-all-start = ((bf16[4,384,640]{2,1,0:T(8,128)(2,1)}), bf16[4,384,640]{2,1,0:T(8,128)(2,1)S(1)}, u32[]{:S(2)}, u32[]{:S(2)}) async-start(bf16[4,384,640]{2,1,0:T(8,128)(2,1)} %repeat.1), calls=%async_computation | async-start | bytes 3932160 | tf_op jit(solution)/shard_map/all_to_all | solution.py:339
  30.3 2.7 %collective-permute-start.13 = (bf16[192,640]{1,0:T(8,128)(2,1)S(1)}, bf16[192,640]{1,0:T(8,128)(2,1)}, u32[]{:S(2)}, u32[]{:S(2)}) collective-permute-start(bf16[192,640]{1,0:T(8,128)(2,1)S(1)} %collective-permute-done.9.refs_8_), channel_id=1, source_target_pairs={{0,28},{4,0},{8,4},{12,8},{16,12},{20,16},{24,20},{28,24},{1,29},{... | collective-permute-start | bytes 737288 | tf_op jit(solution)/shard_map/ppermute | solution.py:324
  33.0 2.7 %collective-permute-start.7 = (bf16[192,640]{1,0:T(8,128)(2,1)}, bf16[192,640]{1,0:T(8,128)(2,1)}, u32[]{:S(2)}, u32[]{:S(2)}) collective-permute-start(bf16[192,640]{1,0:T(8,128)(2,1)} %collective-permute-done.6.refs_13_), channel_id=1, source_target_pairs={{0,28},{4,0},{8,4},{12,8},{16,12},{20,16},{24,20},{28,24},{1,29},{... | collective-permute-start | bytes 737288 | tf_op jit(solution)/shard_map/ppermute | solution.py:324
  36.6 2.7 %collective-permute-start.14 = (bf16[192,640]{1,0:T(8,128)(2,1)}, bf16[192,640]{1,0:T(8,128)(2,1)}, u32[]{:S(2)}, u32[]{:S(2)}) collective-permute-start(bf16[192,640]{1,0:T(8,128)(2,1)} %collective-permute-done.13.refs_10_), channel_id=1, source_target_pairs={{0,28},{4,0},{8,4},{12,8},{16,12},{20,16},{24,20},{28,24},{1,29},{... | collective-permute-start | bytes 737288 | tf_op jit(solution)/shard_map/ppermute | solution.py:324
  41.3 4.9 %collective-permute-done.12.refs_7_ = bf16[192,640]{1,0:T(8,128)(2,1)} collective-permute-done((bf16[192,640]{1,0:T(8,128)(2,1)}, bf16[192,640]{1,0:T(8,128)(2,1)}, u32[]{:S(2)}, u32[]{:S(2)}) %collective-permute-start.12) | collective-permute-done | bytes 245792 | tf_op jit(solution)/shard_map/ppermute | solution.py:324
  46.2 3.9 %all-to-all-done.around_ref = bf16[4,384,640]{2,1,0:T(8,128)(2,1)S(1)} async-done(((bf16[4,384,640]{2,1,0:T(8,128)(2,1)}), bf16[4,384,640]{2,1,0:T(8,128)(2,1)S(1)}, u32[]{:S(2)}, u32[]{:S(2)}) %all-to-all-start) | async-done | bytes 1966112 | tf_op jit(solution)/shard_map/all_to_all | solution.py:339
  51.4 19.4 %attend.1 = bf16[8,208,640]{2,1,0:T(8,128)(2,1)} custom-call(s32[2]{0:T(128)} %last_of.1.place_ref, bf16[192,640]{1,0:T(8,128)(2,1)} %query_ref.1, bf16[4,384,640]{2,1,0:T(8,128)(2,1)} %copy-done.3, bf16[192,640]{1,0:T(8,128)(2,1)} %refs_0_.1, bf16[192,640]{1,0:T(8,128)(2,1)} %refs_1_.1, bf16[192,640]{1,0:T(8,128)(2,1)} %copy-done.7, ...), custom_call_target="tpu_custom_call" | custom-call | flops 24159191040 | tf_op jit(solution)/shard_map/attend/pallas_call | solution.py:162
  70.7 4.4 %all-to-all-start.1 = ((bf16[8,208,640]{2,1,0:T(8,128)(2,1)}), bf16[8,208,640]{2,1,0:T(8,128)(2,1)}, u32[]{:S(2)}, u32[]{:S(2)}) async-start(bf16[8,208,640]{2,1,0:T(8,128)(2,1)} %attend.1), calls=%async_computation.1 | async-start | bytes 4259840 | tf_op jit(solution)/shard_map/all_to_all | solution.py:354
  75.2 2.9 %copy-done = bf16[640,5120]{1,0:T(8,128)(2,1)S(1)} copy-done((bf16[640,5120]{1,0:T(8,128)(2,1)S(1)}, bf16[640,5120]{1,0:T(8,128)(2,1)}, u32[]{:S(2)}) %copy-start) | copy-done | bytes 6553624
  79.1 17.5 %all-to-all-done.1.refs_0_ = bf16[8,208,640]{2,1,0:T(8,128)(2,1)} async-done(((bf16[8,208,640]{2,1,0:T(8,128)(2,1)}), bf16[8,208,640]{2,1,0:T(8,128)(2,1)}, u32[]{:S(2)}, u32[]{:S(2)}) %all-to-all-start.1) | async-done | bytes 2129952 | tf_op jit(solution)/shard_map/all_to_all | solution.py:354
  96.6 4.8 %combine.1 = (bf16[192,640]{1,0:T(8,128)(2,1)S(1)}, bf16[192,1280]{1,0:T(8,128)(2,1)S(1)}, bf16[192,1280]{1,0:T(8,128)(2,1)}) custom-call(bf16[2,640,1280]{2,1,0:T(8,128)(2,1)S(1)} %select_columns.2.w_ref, bf16[8,208,640]{2,1,0:T(8,128)(2,1)} %all-to-all-done.1.refs_0_), custom_call_target="tpu_custom_call" | custom-call | tf_op jit(solution)/shard_map/combine/pallas_call | solution.py:266
  101.3 6.9 %collective-permute-start.15 = (bf16[192,1280]{1,0:T(8,128)(2,1)S(1)}, bf16[192,1280]{1,0:T(8,128)(2,1)S(1)}, u32[]{:S(2)}, u32[]{:S(2)}) collective-permute-start(bf16[192,1280]{1,0:T(8,128)(2,1)S(1)} %get-tuple-element.18), channel_id=1, source_target_pairs={{0,1},{1,0},{2,3},{3,2},{4,5},{5,4},{6,7},{7,6},{8,9},{9,8},{10,11... | collective-permute-start | bytes 1474568 | tf_op jit(solution)/shard_map/ppermute | solution.py:365
  108.2 2.9 %copy-done.1 = bf16[640,5120]{1,0:T(8,128)(2,1)S(1)} copy-done((bf16[640,5120]{1,0:T(8,128)(2,1)S(1)}, bf16[640,5120]{1,0:T(8,128)(2,1)}, u32[]{:S(2)}) %copy-start.1) | copy-done | bytes 6553624
  112.5 2.8 %collective-permute-start.17 = (bf16[192,1280]{1,0:T(8,128)(2,1)S(1)}, bf16[192,1280]{1,0:T(8,128)(2,1)S(1)}, u32[]{:S(2)}, u32[]{:S(2)}) collective-permute-start(bf16[192,1280]{1,0:T(8,128)(2,1)S(1)} %add_convert_fusion.1), channel_id=1, source_target_pairs={{0,2},{2,0},{1,3},{3,1},{4,6},{6,4},{5,7},{7,5},{8,10},{10,8},{9,1... | collective-permute-start | bytes 1474568 | tf_op jit(solution)/shard_map/ppermute | solution.py:368
  115.3 2.9 %copy-done.2 = bf16[640,5120]{1,0:T(8,128)(2,1)S(1)} copy-done((bf16[640,5120]{1,0:T(8,128)(2,1)S(1)}, bf16[640,5120]{1,0:T(8,128)(2,1)}, u32[]{:S(2)}) %copy-start.2) | copy-done | bytes 6553624
  119.5 7.0 %collective-permute-done.17 = bf16[192,1280]{1,0:T(8,128)(2,1)S(1)} collective-permute-done((bf16[192,1280]{1,0:T(8,128)(2,1)S(1)}, bf16[192,1280]{1,0:T(8,128)(2,1)S(1)}, u32[]{:S(2)}, u32[]{:S(2)}) %collective-permute-start.17) | collective-permute-done | bytes 491552 | tf_op jit(solution)/shard_map/ppermute | solution.py:368
  (56 shorter events, 11.0 us)
Async XLA Ops:
  0.0 12.3 %collective-permute-start = (bf16[192,640]{1,0:T(8,128)(2,1)}, bf16[192,640]{1,0:T(8,128)(2,1)S(1)}, u32[]{:S(2)}, u32[]{:S(2)}) collective-permute-start(bf16[192,640]{1,0:T(8,128)(2,1)} %refs_0_.1), channel_id=1, source_target_pairs={{0,4},{4,8},{8,12},{12,16},{16,20},{20,24},{24,28},{28,0},{1,5},{5... | collective-permute-start | bytes 737288 | tf_op jit(solution)/shard_map/ppermute | solution.py:324
  2.5 9.8 %collective-permute-start.4 = (bf16[192,640]{1,0:T(8,128)(2,1)}, bf16[192,640]{1,0:T(8,128)(2,1)S(1)}, u32[]{:S(2)}, u32[]{:S(2)}) collective-permute-start(bf16[192,640]{1,0:T(8,128)(2,1)} %refs_1_.1), channel_id=1, source_target_pairs={{0,28},{4,0},{8,4},{12,8},{16,12},{20,16},{24,20},{28,24},{1,29},{... | collective-permute-start | bytes 737288 | tf_op jit(solution)/shard_map/ppermute | solution.py:324
  12.3 29.0 %copy-start.7 = (bf16[192,640]{1,0:T(8,128)(2,1)}, bf16[192,640]{1,0:T(8,128)(2,1)S(1)}, u32[]{:S(2)}) copy-start(bf16[192,640]{1,0:T(8,128)(2,1)S(1)} %collective-permute-done.refs_2_) | copy-start | bytes 737284
  12.3 7.4 %collective-permute-start.1 = (bf16[192,640]{1,0:T(8,128)(2,1)S(1)}, bf16[192,640]{1,0:T(8,128)(2,1)S(1)}, u32[]{:S(2)}, u32[]{:S(2)}) collective-permute-start(bf16[192,640]{1,0:T(8,128)(2,1)S(1)} %collective-permute-done.refs_2_), channel_id=1, source_target_pairs={{0,4},{4,8},{8,12},{12,16},{16,20},{20,24},{24,28},{28,0},{1,5},{5... | collective-permute-start | bytes 737288 | tf_op jit(solution)/shard_map/ppermute | solution.py:324
  12.3 29.0 %copy-start.8 = (bf16[192,640]{1,0:T(8,128)(2,1)}, bf16[192,640]{1,0:T(8,128)(2,1)S(1)}, u32[]{:S(2)}) copy-start(bf16[192,640]{1,0:T(8,128)(2,1)S(1)} %collective-permute-done.4.refs_9_) | copy-start | bytes 737284
  12.3 7.4 %collective-permute-start.5 = (bf16[192,640]{1,0:T(8,128)(2,1)S(1)}, bf16[192,640]{1,0:T(8,128)(2,1)S(1)}, u32[]{:S(2)}, u32[]{:S(2)}) collective-permute-start(bf16[192,640]{1,0:T(8,128)(2,1)S(1)} %collective-permute-done.4.refs_9_), channel_id=1, source_target_pairs={{0,28},{4,0},{8,4},{12,8},{16,12},{20,16},{24,20},{28,24},{1,29},{... | collective-permute-start | bytes 737288 | tf_op jit(solution)/shard_map/ppermute | solution.py:324
  15.0 7.4 %collective-permute-start.8 = (bf16[192,640]{1,0:T(8,128)(2,1)}, bf16[192,640]{1,0:T(8,128)(2,1)S(1)}, u32[]{:S(2)}, u32[]{:S(2)}) collective-permute-start(bf16[192,640]{1,0:T(8,128)(2,1)} %query_ref.1), channel_id=1, source_target_pairs={{0,32},{32,0},{1,33},{33,1},{2,34},{34,2},{3,35},{35,3},{4,36},{36... | collective-permute-start | bytes 737288 | tf_op jit(solution)/shard_map/ppermute | solution.py:332
  16.2 9.8 %collective-permute-start.9 = (bf16[192,640]{1,0:T(8,128)(2,1)}, bf16[192,640]{1,0:T(8,128)(2,1)S(1)}, u32[]{:S(2)}, u32[]{:S(2)}) collective-permute-start(bf16[192,640]{1,0:T(8,128)(2,1)} %refs_0_.1), channel_id=1, source_target_pairs={{0,28},{4,0},{8,4},{12,8},{16,12},{20,16},{24,20},{28,24},{1,29},{... | collective-permute-start | bytes 737288 | tf_op jit(solution)/shard_map/ppermute | solution.py:324
  16.3 13.9 %collective-permute-start.10 = (bf16[192,640]{1,0:T(8,128)(2,1)}, bf16[192,640]{1,0:T(8,128)(2,1)S(1)}, u32[]{:S(2)}, u32[]{:S(2)}) collective-permute-start(bf16[192,640]{1,0:T(8,128)(2,1)} %refs_1_.1), channel_id=1, source_target_pairs={{0,4},{4,8},{8,12},{12,16},{16,20},{20,24},{24,28},{28,0},{1,5},{5... | collective-permute-start | bytes 737288 | tf_op jit(solution)/shard_map/ppermute | solution.py:324
  19.7 21.6 %copy-start.9 = (bf16[192,640]{1,0:T(8,128)(2,1)}, bf16[192,640]{1,0:T(8,128)(2,1)S(1)}, u32[]{:S(2)}) copy-start(bf16[192,640]{1,0:T(8,128)(2,1)S(1)} %collective-permute-done.1.refs_4_) | copy-start | bytes 737284
  19.7 13.2 %collective-permute-start.2 = (bf16[192,640]{1,0:T(8,128)(2,1)S(1)}, bf16[192,640]{1,0:T(8,128)(2,1)}, u32[]{:S(2)}, u32[]{:S(2)}) collective-permute-start(bf16[192,640]{1,0:T(8,128)(2,1)S(1)} %collective-permute-done.1.refs_4_), channel_id=1, source_target_pairs={{0,4},{4,8},{8,12},{12,16},{16,20},{20,24},{24,28},{28,0},{1,5},{5... | collective-permute-start | bytes 737288 | tf_op jit(solution)/shard_map/ppermute | solution.py:324
  19.7 21.6 %copy-start.10 = (bf16[192,640]{1,0:T(8,128)(2,1)}, bf16[192,640]{1,0:T(8,128)(2,1)S(1)}, u32[]{:S(2)}) copy-start(bf16[192,640]{1,0:T(8,128)(2,1)S(1)} %collective-permute-done.5.refs_11_) | copy-start | bytes 737284
  19.8 13.2 %collective-permute-start.6 = (bf16[192,640]{1,0:T(8,128)(2,1)S(1)}, bf16[192,640]{1,0:T(8,128)(2,1)}, u32[]{:S(2)}, u32[]{:S(2)}) collective-permute-start(bf16[192,640]{1,0:T(8,128)(2,1)S(1)} %collective-permute-done.5.refs_11_), channel_id=1, source_target_pairs={{0,28},{4,0},{8,4},{12,8},{16,12},{20,16},{24,20},{28,24},{1,29},{... | collective-permute-start | bytes 737288 | tf_op jit(solution)/shard_map/ppermute | solution.py:324
  26.0 24.1 %all-to-all-start = ((bf16[4,384,640]{2,1,0:T(8,128)(2,1)}), bf16[4,384,640]{2,1,0:T(8,128)(2,1)S(1)}, u32[]{:S(2)}, u32[]{:S(2)}) async-start(bf16[4,384,640]{2,1,0:T(8,128)(2,1)} %repeat.1), calls=%async_computation | async-start | bytes 3932160 | tf_op jit(solution)/shard_map/all_to_all | solution.py:339
  30.2 6.4 %collective-permute-start.11 = (bf16[192,640]{1,0:T(8,128)(2,1)S(1)}, bf16[192,640]{1,0:T(8,128)(2,1)}, u32[]{:S(2)}, u32[]{:S(2)}) collective-permute-start(bf16[192,640]{1,0:T(8,128)(2,1)S(1)} %collective-permute-done.10.refs_3_), channel_id=1, source_target_pairs={{0,4},{4,8},{8,12},{12,16},{16,20},{20,24},{24,28},{28,0},{1,5},{5... | collective-permute-start | bytes 737288 | tf_op jit(solution)/shard_map/ppermute | solution.py:324
  30.3 6.4 %collective-permute-start.13 = (bf16[192,640]{1,0:T(8,128)(2,1)S(1)}, bf16[192,640]{1,0:T(8,128)(2,1)}, u32[]{:S(2)}, u32[]{:S(2)}) collective-permute-start(bf16[192,640]{1,0:T(8,128)(2,1)S(1)} %collective-permute-done.9.refs_8_), channel_id=1, source_target_pairs={{0,28},{4,0},{8,4},{12,8},{16,12},{20,16},{24,20},{28,24},{1,29},{... | collective-permute-start | bytes 737288 | tf_op jit(solution)/shard_map/ppermute | solution.py:324
  32.9 7.1 %collective-permute-start.3 = (bf16[192,640]{1,0:T(8,128)(2,1)}, bf16[192,640]{1,0:T(8,128)(2,1)}, u32[]{:S(2)}, u32[]{:S(2)}) collective-permute-start(bf16[192,640]{1,0:T(8,128)(2,1)} %collective-permute-done.2.refs_6_), channel_id=1, source_target_pairs={{0,4},{4,8},{8,12},{12,16},{16,20},{20,24},{24,28},{28,0},{1,5},{5... | collective-permute-start | bytes 737288 | tf_op jit(solution)/shard_map/ppermute | solution.py:324
  33.0 7.1 %collective-permute-start.7 = (bf16[192,640]{1,0:T(8,128)(2,1)}, bf16[192,640]{1,0:T(8,128)(2,1)}, u32[]{:S(2)}, u32[]{:S(2)}) collective-permute-start(bf16[192,640]{1,0:T(8,128)(2,1)} %collective-permute-done.6.refs_13_), channel_id=1, source_target_pairs={{0,28},{4,0},{8,4},{12,8},{16,12},{20,16},{24,20},{28,24},{1,29},{... | collective-permute-start | bytes 737288 | tf_op jit(solution)/shard_map/ppermute | solution.py:324
  36.6 9.5 %collective-permute-start.12 = (bf16[192,640]{1,0:T(8,128)(2,1)}, bf16[192,640]{1,0:T(8,128)(2,1)}, u32[]{:S(2)}, u32[]{:S(2)}) collective-permute-start(bf16[192,640]{1,0:T(8,128)(2,1)} %collective-permute-done.11.refs_5_), channel_id=1, source_target_pairs={{0,4},{4,8},{8,12},{12,16},{16,20},{20,24},{24,28},{28,0},{1,5},{5... | collective-permute-start | bytes 737288 | tf_op jit(solution)/shard_map/ppermute | solution.py:324
  36.6 9.5 %collective-permute-start.14 = (bf16[192,640]{1,0:T(8,128)(2,1)}, bf16[192,640]{1,0:T(8,128)(2,1)}, u32[]{:S(2)}, u32[]{:S(2)}) collective-permute-start(bf16[192,640]{1,0:T(8,128)(2,1)} %collective-permute-done.13.refs_10_), channel_id=1, source_target_pairs={{0,28},{4,0},{8,4},{12,8},{16,12},{20,16},{24,20},{28,24},{1,29},{... | collective-permute-start | bytes 737288 | tf_op jit(solution)/shard_map/ppermute | solution.py:324
  70.7 25.8 %all-to-all-start.1 = ((bf16[8,208,640]{2,1,0:T(8,128)(2,1)}), bf16[8,208,640]{2,1,0:T(8,128)(2,1)}, u32[]{:S(2)}, u32[]{:S(2)}) async-start(bf16[8,208,640]{2,1,0:T(8,128)(2,1)} %attend.1), calls=%async_computation.1 | async-start | bytes 4259840 | tf_op jit(solution)/shard_map/all_to_all | solution.py:354
  101.3 10.9 %collective-permute-start.15 = (bf16[192,1280]{1,0:T(8,128)(2,1)S(1)}, bf16[192,1280]{1,0:T(8,128)(2,1)S(1)}, u32[]{:S(2)}, u32[]{:S(2)}) collective-permute-start(bf16[192,1280]{1,0:T(8,128)(2,1)S(1)} %get-tuple-element.18), channel_id=1, source_target_pairs={{0,1},{1,0},{2,3},{3,2},{4,5},{5,4},{6,7},{7,6},{8,9},{9,8},{10,11... | collective-permute-start | bytes 1474568 | tf_op jit(solution)/shard_map/ppermute | solution.py:365
  112.4 6.9 %collective-permute-start.16 = (bf16[192,1280]{1,0:T(8,128)(2,1)}, bf16[192,1280]{1,0:T(8,128)(2,1)S(1)}, u32[]{:S(2)}, u32[]{:S(2)}) collective-permute-start(bf16[192,1280]{1,0:T(8,128)(2,1)} %get-tuple-element.20), channel_id=1, source_target_pairs={{0,1},{1,0},{2,3},{3,2},{4,5},{5,4},{6,7},{7,6},{8,9},{9,8},{10,11... | collective-permute-start | bytes 1474568 | tf_op jit(solution)/shard_map/ppermute | solution.py:370
  112.5 14.0 %collective-permute-start.17 = (bf16[192,1280]{1,0:T(8,128)(2,1)S(1)}, bf16[192,1280]{1,0:T(8,128)(2,1)S(1)}, u32[]{:S(2)}, u32[]{:S(2)}) collective-permute-start(bf16[192,1280]{1,0:T(8,128)(2,1)S(1)} %add_convert_fusion.1), channel_id=1, source_target_pairs={{0,2},{2,0},{1,3},{3,1},{4,6},{6,4},{5,7},{7,5},{8,10},{10,8},{9,1... | collective-permute-start | bytes 1474568 | tf_op jit(solution)/shard_map/ppermute | solution.py:368
  (9 other events, 39.4 us)
